TPU v7x, 256 devices: a whole 4x4x8 slice. The times are simulated.
256 devices in a mesh: ctx: 64 (over y, x, z_lo, core), head: 4 (over z_hi).
Axes of the slice: x: 4, y: 4, z: 8 (z_hi: 4, z_lo: 2; z = z_hi * 2 + z_lo), core: 2. Of those that a mesh axis runs over, the one named last changes fastest.
Arguments:
- query: bfloat16 [8192, 3072], P('ctx', 'head'), may hold values from -8 to 8
- latent: bfloat16 [8192, 512], P('ctx'), may hold values from -16 to 16
- k_rope: bfloat16 [8192, 64], P('ctx'), may hold values from -8 to 8
- d_out: bfloat16 [8192, 2048], P('ctx', 'head'), may hold values from -6 to 6
- w_kv: bfloat16 [512, 4096], P(None, 'head'), may hold values from -0.25 to 0.25
- block_doc: int32 [64], replicated, may hold values from 0 to 7, never falling along the last dimension, each value on 1 to 36 neighbouring positions
- block_order: int32 [64], replicated, may hold values from 0 to 63, as said below
Outputs:
- d_query: bfloat16 [8192, 3072], P('ctx', 'head')
- d_latent: float32 [8192, 512], P('ctx')
- d_rope: float32 [8192, 64], P('ctx')
- d_w_kv: float32 [512, 4096], P('ctx', 'head')
Inputs may be any that keep to these rules, and one draw needn't show every extreme that they name: block_doc never falls along the sequence; every document is a run of 1 to 36 whole blocks and one has exactly 36. `block_order`: each sequence block stands in exactly one slot; the slots of each aligned group of 4 slots hold exactly the sequence blocks of the same indices, in some order.
All inputs are finite; a program needn't handle non-finite values.
Results may differ from a plain program's by a relative error of at most 0.0073.
Values may be sent and summed in bfloat16 or wider, within the bound.
A program may use at most 128 MiB of HBM per device.

v0:
```python
import jax
import jax.numpy as jnp
from jax import lax
from jax.sharding import PartitionSpec as P

LAT = 512
ROPE = 64
NOPE = 128
VDIM = 128
BLK = 128


big_negative = -1e30


def table_lookup(indices, lookup_table):
    entries = lookup_table.shape[0]
    matches = indices[:, None] == jnp.arange(entries, dtype=jnp.int32)[None, :]
    return jnp.sum(jnp.where(matches, lookup_table[None, :], 0), axis=1)


def inverse_order(block_order):
    entries = block_order.shape[0]
    positions = jnp.arange(entries, dtype=jnp.int32)
    matches = block_order[None, :] == positions[:, None]
    return jnp.sum(jnp.where(matches, positions[None, :], 0), axis=1)


def local(query, latent, k_rope, d_out, w_kv, block_doc, block_order):
    row_count = query.shape[0]
    head_width = NOPE + ROPE
    pair_width = NOPE + VDIM
    head_count = query.shape[1] // head_width
    kv_width = w_kv.shape[1]
    score_scale = head_width ** (-0.5)
    block_count = block_order.shape[0]
    token_count = block_count * BLK
    key_span = 4 * BLK
    feat_width = LAT + ROPE
    own_blocks = row_count // BLK
    my_index = lax.axis_index("ctx")
    own_order = lax.dynamic_slice_in_dim(block_order, my_index * own_blocks, own_blocks)
    offsets = jnp.arange(BLK, dtype=jnp.int32)
    query_pos = (own_order[:, None] * BLK + offsets[None, :]).reshape(row_count)
    query_doc = jnp.repeat(table_lookup(own_order, block_doc), BLK)
    query_parts = query.reshape(row_count, head_count, head_width)
    query_nope = query_parts[:, :, :NOPE]
    query_rope = query_parts[:, :, NOPE:]
    grad_out = d_out.reshape(row_count, head_count, VDIM)
    packed = jnp.concatenate([latent, k_rope], axis=1).reshape(row_count // 2, 2 * feat_width)
    gathered = lax.all_gather(packed, "ctx", axis=0, tiled=True)
    in_sequence = jnp.take(
        gathered.reshape(block_count, BLK, feat_width), inverse_order(block_order), axis=0
    )
    in_sequence = in_sequence.reshape(token_count, feat_width)
    key_pos = jnp.arange(token_count, dtype=jnp.int32)
    key_doc = jnp.repeat(block_doc, BLK)
    all_latent = in_sequence[:, :LAT]
    all_rope = in_sequence[:, LAT:]
    step_count = all_latent.shape[0] // key_span

    def allowed_at(step_index):
        key_start = step_index * key_span
        docs_here = lax.dynamic_slice_in_dim(key_doc, key_start, key_span)
        pos_here = lax.dynamic_slice_in_dim(key_pos, key_start, key_span)
        return (query_doc[:, None] == docs_here[None, :]) & (
            pos_here[None, :] <= query_pos[:, None]
        )

    def rows_at(step_index):
        key_start = step_index * key_span
        lat_rows = lax.dynamic_slice_in_dim(all_latent, key_start, key_span, 0)
        rope_rows = lax.dynamic_slice_in_dim(all_rope, key_start, key_span, 0)
        return (lat_rows, rope_rows)

    def split_pairs(key_value):
        key_value = key_value.reshape(key_span, head_count, pair_width)
        return (key_value[:, :, :NOPE], key_value[:, :, NOPE:])

    def scores_of(rope_rows, keys_here):
        scores = jnp.einsum(
            "qhd,khd->hqk", query_nope, keys_here, preferred_element_type=jnp.float32
        )
        scores = scores + jnp.einsum(
            "qhd,kd->hqk", query_rope, rope_rows, preferred_element_type=jnp.float32
        )
        return score_scale * scores

    def stats_step(carried, step_index):
        allowed = allowed_at(step_index)

        def stats_live_step(state):
            row_max, mass, weighted = state
            lat_rows, rope_rows = rows_at(step_index)
            key_value = jnp.dot(lat_rows, w_kv, preferred_element_type=jnp.float32).astype(
                jnp.bfloat16
            )
            keys_here, values_here = split_pairs(key_value)
            scores = scores_of(rope_rows, keys_here)
            d_probs = jnp.einsum(
                "qhd,khd->hqk", grad_out, values_here, preferred_element_type=jnp.float32
            )
            new_max = jnp.maximum(
                row_max, jnp.max(jnp.where(allowed[None], scores, big_negative), axis=2)
            )
            weights = jnp.where(allowed[None], jnp.exp(scores - new_max[:, :, None]), 0.0)
            shrink = jnp.exp(row_max - new_max)
            new_state = (
                new_max,
                mass * shrink + jnp.sum(weights, axis=2),
                weighted * shrink + jnp.sum(weights * d_probs, axis=2),
            )
            return (new_state, key_value)

        def stats_dead_step(state):
            return (state, jnp.zeros((key_span, kv_width), jnp.bfloat16))

        return lax.cond(jnp.any(allowed), stats_live_step, stats_dead_step, carried)

    start_state = (
        jnp.full((head_count, row_count), big_negative, jnp.float32),
        jnp.zeros((head_count, row_count), jnp.float32),
        jnp.zeros((head_count, row_count), jnp.float32),
    )
    (row_max, mass, weighted), kv_steps = lax.scan(stats_step, start_state, jnp.arange(step_count))
    delta = weighted / mass

    def grad_step(carried, inputs):
        step_index, key_value = inputs
        allowed = allowed_at(step_index)

        def grad_live_step(state):
            dq_nope, dq_rope, weight_grad = state
            lat_rows, rope_rows = rows_at(step_index)
            keys_here, values_here = split_pairs(key_value)
            scores = scores_of(rope_rows, keys_here)
            probs = jnp.where(
                allowed[None], jnp.exp(scores - row_max[:, :, None]) / mass[:, :, None], 0.0
            )
            d_probs = jnp.einsum(
                "qhd,khd->hqk", grad_out, values_here, preferred_element_type=jnp.float32
            )
            mixed = (probs * (d_probs - delta[:, :, None])).astype(jnp.bfloat16)
            probs_b = probs.astype(jnp.bfloat16)
            dq_nope = dq_nope + score_scale * jnp.einsum(
                "hqk,khd->qhd", mixed, keys_here, preferred_element_type=jnp.float32
            )
            dq_rope = dq_rope + score_scale * jnp.einsum(
                "hqk,kd->qhd", mixed, rope_rows, preferred_element_type=jnp.float32
            )
            d_keys = score_scale * jnp.einsum(
                "hqk,qhd->khd", mixed, query_nope, preferred_element_type=jnp.float32
            )
            d_values = jnp.einsum(
                "hqk,qhd->khd", probs_b, grad_out, preferred_element_type=jnp.float32
            )
            d_rope_rows = score_scale * jnp.einsum(
                "hqk,qhd->kd", mixed, query_rope, preferred_element_type=jnp.float32
            )
            d_pairs = jnp.concatenate([d_keys, d_values], axis=2).astype(jnp.bfloat16)
            d_pairs = d_pairs.reshape(key_span, kv_width)
            d_lat_rows = lax.dot_general(
                d_pairs, w_kv, (((1,), (1,)), ((), ())), preferred_element_type=jnp.float32
            )
            weight_grad = weight_grad + lax.dot_general(
                lat_rows, d_pairs, (((0,), (0,)), ((), ())), preferred_element_type=jnp.float32
            )
            return (
                (dq_nope, dq_rope, weight_grad),
                jnp.concatenate([d_lat_rows, d_rope_rows], axis=1),
            )

        def grad_dead_step(state):
            return (state, jnp.zeros((key_span, feat_width), jnp.float32))

        return lax.cond(jnp.any(allowed), grad_live_step, grad_dead_step, carried)

    start_grads = (
        jnp.zeros((row_count, head_count, NOPE), jnp.float32),
        jnp.zeros((row_count, head_count, ROPE), jnp.float32),
        jnp.zeros((LAT, kv_width), jnp.float32),
    )
    (dq_nope, dq_rope, weight_grad), term_rows = lax.scan(
        grad_step, start_grads, (jnp.arange(step_count), kv_steps)
    )
    d_query = jnp.concatenate([dq_nope, dq_rope], axis=2).astype(jnp.bfloat16)
    d_query = d_query.reshape(row_count, head_count * head_width)
    d_query, weight_grad, term_rows = (
        d_query,
        weight_grad,
        term_rows.reshape(step_count * key_span, feat_width),
    )
    slot_terms = jnp.take(term_rows.reshape(block_count, BLK, feat_width), block_order, axis=0)
    slot_terms = slot_terms.reshape(token_count // 2, 2 * feat_width)
    shard_sum = lax.psum_scatter(slot_terms, "ctx", scatter_dimension=0, tiled=True)
    own_rows = lax.psum(shard_sum, "head")
    own_rows = own_rows.reshape(row_count, feat_width)
    d_latent = own_rows[:, :LAT]
    d_rope = own_rows[:, LAT:]
    d_w_kv = lax.psum_scatter(weight_grad, "ctx", scatter_dimension=0, tiled=True)
    return (d_query, d_latent, d_rope, d_w_kv)


def solution(mesh):
    return jax.shard_map(
        local,
        mesh=mesh,
        in_specs=(
            P("ctx", "head"),
            P("ctx", None),
            P("ctx", None),
            P("ctx", "head"),
            P(None, "head"),
            P(),
            P(),
        ),
        out_specs=(P("ctx", "head"), P("ctx", None), P("ctx", None), P("ctx", "head")),
        check_vma=False,
    )
```

profile of v0, /device:TPU:64, one launch (start us, length us, event | category | flops | bytes accessed | tf_op | source)
XLA Modules:
  0.0 1704.6 jit_solution(10544123869101215934)
XLA Ops:
  15.7 1.9 fusion.51
  19.1 109.4 %all-gather.2.cloned.1.call-done = bf16[4096,1152]{1,0:T(8,128)(2,1)} async-done(((bf16[64,1152]{1,0:T(8,128)(2,1)}), bf16[4096,1152]{1,0:T(8,128)(2,1)}) %all-gather.2.cloned.1.call-update) | async-done | bytes 9437200 | tf_op jit(solution)/shard_map/all_gather | solution.py:51
  128.5 17.3 %reshape.111 = bf16[64,128,576]{2,1,0:T(8,128)(2,1)} reshape(bf16[4096,1152]{1,0:T(8,128)(2,1)} %all-gather.2.cloned.1.call-done) | data formatting | bytes 18874368 | tf_op jit(solution)/shard_map/reshape | solution.py:53
  145.8 10.6 gather_fusion
  156.4 11.6 bitcast_select_fusion
  168.0 7.4 slice.46
  175.3 1.6 copy.94
  177.0 121.6 %while.34 = (s32[]{:T(128)}, f32[4,128]{1,0:T(4,128)S(1)}, f32[4,128]{1,0:T(4,128)S(1)}, f32[4,128]{1,0:T(4,128)S(1)}, bf16[16,512,1024]{1,2,0:T(8,128)(2,1)}, /...) while((s32[]{:T(128)}, f32[4,128]{1,0:T(4,128)S(1)}, ...), condition=%wide.region_9.10_spmd.clone, body=%wide.region_2.9_spmd.clone.sunk | while | flops 708249728 | bytes 18004940 | solution.py:125
  180.4 8.2 conditional.6
  181.1 3.1 convolution_convert_fusion
  184.2 1.9 reshape.101
  188.6 1.5 copy.125
  195.7 1.5 copy.125
  202.9 1.5 copy.125
  210.0 1.5 copy.125
  238.7 1.5 copy.125
  260.2 1.5 copy.125
  298.6 1.6 broadcast_in_dim.132
  300.2 477.0 %while.35 = (s32[]{:T(128)}, f32[128,4,128]{2,0,1:T(8,128)S(1)}, f32[128,4,64]{0,2,1:T(8,128)S(1)}, f32[512,1024]{1,0:T(8,128)}, f32[16,512,576]{1,0,2:T(8,128)}...) while((s32[]{:T(128)}, f32[128,4,128]{2,0,1:T(8,128)S(1)}, ...), condition=%wide.region_14.15_spmd.clone, body=%wide.region_10.14_spmd.clone.sunk | while | flops 1516438144 | bytes 36717116 | solution.py:183
  303.8 11.2 conditional.7
  309.7 3.9 convolution_add_fusion
  316.2 24.3 %dynamic_update_slice.14 = f32[16,512,576]{1,0,2:T(8,128)} dynamic-update-slice(f32[16,512,576]{1,0,2:T(8,128)} %get-tuple-element.1024, f32[1,512,576]{1,0,2:T(1,128)S(1)} %copy.126, s32[]{:T(128)} %get-tuple-element.1020, s32[]{:T(128)} %constant.90.clone.1..sunk.1, s32[]{:T(128)} %constant.90.clone.1..sunk.1) | dynamic-update-slice | bytes 2359300 | tf_op jit(solution)/shard_map/while/body/jit(dynamic_update_index_in_dim)/dynamic_update_slice | solution.py:183
  345.3 24.3 %dynamic_update_slice.14 = f32[16,512,576]{1,0,2:T(8,128)} dynamic-update-slice(f32[16,512,576]{1,0,2:T(8,128)} %get-tuple-element.1024, f32[1,512,576]{1,0,2:T(1,128)S(1)} %copy.126, s32[]{:T(128)} %get-tuple-element.1020, s32[]{:T(128)} %constant.90.clone.1..sunk.1, s32[]{:T(128)} %constant.90.clone.1..sunk.1) | dynamic-update-slice | bytes 2359300 | tf_op jit(solution)/shard_map/while/body/jit(dynamic_update_index_in_dim)/dynamic_update_slice | solution.py:183
  374.4 24.3 %dynamic_update_slice.14 = f32[16,512,576]{1,0,2:T(8,128)} dynamic-update-slice(f32[16,512,576]{1,0,2:T(8,128)} %get-tuple-element.1024, f32[1,512,576]{1,0,2:T(1,128)S(1)} %copy.126, s32[]{:T(128)} %get-tuple-element.1020, s32[]{:T(128)} %constant.90.clone.1..sunk.1, s32[]{:T(128)} %constant.90.clone.1..sunk.1) | dynamic-update-slice | bytes 2359300 | tf_op jit(solution)/shard_map/while/body/jit(dynamic_update_index_in_dim)/dynamic_update_slice | solution.py:183
  403.5 24.3 %dynamic_update_slice.14 = f32[16,512,576]{1,0,2:T(8,128)} dynamic-update-slice(f32[16,512,576]{1,0,2:T(8,128)} %get-tuple-element.1024, f32[1,512,576]{1,0,2:T(1,128)S(1)} %copy.126, s32[]{:T(128)} %get-tuple-element.1020, s32[]{:T(128)} %constant.90.clone.1..sunk.1, s32[]{:T(128)} %constant.90.clone.1..sunk.1) | dynamic-update-slice | bytes 2359300 | tf_op jit(solution)/shard_map/while/body/jit(dynamic_update_index_in_dim)/dynamic_update_slice | solution.py:183
  432.6 24.3 %dynamic_update_slice.14 = f32[16,512,576]{1,0,2:T(8,128)} dynamic-update-slice(f32[16,512,576]{1,0,2:T(8,128)} %get-tuple-element.1024, f32[1,512,576]{1,0,2:T(1,128)S(1)} %copy.126, s32[]{:T(128)} %get-tuple-element.1020, s32[]{:T(128)} %constant.90.clone.1..sunk.1, s32[]{:T(128)} %constant.90.clone.1..sunk.1) | dynamic-update-slice | bytes 2359300 | tf_op jit(solution)/shard_map/while/body/jit(dynamic_update_index_in_dim)/dynamic_update_slice | solution.py:183
  461.7 24.3 %dynamic_update_slice.14 = f32[16,512,576]{1,0,2:T(8,128)} dynamic-update-slice(f32[16,512,576]{1,0,2:T(8,128)} %get-tuple-element.1024, f32[1,512,576]{1,0,2:T(1,128)S(1)} %copy.126, s32[]{:T(128)} %get-tuple-element.1020, s32[]{:T(128)} %constant.90.clone.1..sunk.1, s32[]{:T(128)} %constant.90.clone.1..sunk.1) | dynamic-update-slice | bytes 2359300 | tf_op jit(solution)/shard_map/while/body/jit(dynamic_update_index_in_dim)/dynamic_update_slice | solution.py:183
  490.8 24.3 %dynamic_update_slice.14 = f32[16,512,576]{1,0,2:T(8,128)} dynamic-update-slice(f32[16,512,576]{1,0,2:T(8,128)} %get-tuple-element.1024, f32[1,512,576]{1,0,2:T(1,128)S(1)} %copy.126, s32[]{:T(128)} %get-tuple-element.1020, s32[]{:T(128)} %constant.90.clone.1..sunk.1, s32[]{:T(128)} %constant.90.clone.1..sunk.1) | dynamic-update-slice | bytes 2359300 | tf_op jit(solution)/shard_map/while/body/jit(dynamic_update_index_in_dim)/dynamic_update_slice | solution.py:183
  519.9 24.3 %dynamic_update_slice.14 = f32[16,512,576]{1,0,2:T(8,128)} dynamic-update-slice(f32[16,512,576]{1,0,2:T(8,128)} %get-tuple-element.1024, f32[1,512,576]{1,0,2:T(1,128)S(1)} %copy.126, s32[]{:T(128)} %get-tuple-element.1020, s32[]{:T(128)} %constant.90.clone.1..sunk.1, s32[]{:T(128)} %constant.90.clone.1..sunk.1) | dynamic-update-slice | bytes 2359300 | tf_op jit(solution)/shard_map/while/body/jit(dynamic_update_index_in_dim)/dynamic_update_slice | solution.py:183
  549.0 24.3 %dynamic_update_slice.14 = f32[16,512,576]{1,0,2:T(8,128)} dynamic-update-slice(f32[16,512,576]{1,0,2:T(8,128)} %get-tuple-element.1024, f32[1,512,576]{1,0,2:T(1,128)S(1)} %copy.126, s32[]{:T(128)} %get-tuple-element.1020, s32[]{:T(128)} %constant.90.clone.1..sunk.1, s32[]{:T(128)} %constant.90.clone.1..sunk.1) | dynamic-update-slice | bytes 2359300 | tf_op jit(solution)/shard_map/while/body/jit(dynamic_update_index_in_dim)/dynamic_update_slice | solution.py:183
  578.1 24.3 %dynamic_update_slice.14 = f32[16,512,576]{1,0,2:T(8,128)} dynamic-update-slice(f32[16,512,576]{1,0,2:T(8,128)} %get-tuple-element.1024, f32[1,512,576]{1,0,2:T(1,128)S(1)} %copy.126, s32[]{:T(128)} %get-tuple-element.1020, s32[]{:T(128)} %constant.90.clone.1..sunk.1, s32[]{:T(128)} %constant.90.clone.1..sunk.1) | dynamic-update-slice | bytes 2359300 | tf_op jit(solution)/shard_map/while/body/jit(dynamic_update_index_in_dim)/dynamic_update_slice | solution.py:183
  607.3 24.3 %dynamic_update_slice.14 = f32[16,512,576]{1,0,2:T(8,128)} dynamic-update-slice(f32[16,512,576]{1,0,2:T(8,128)} %get-tuple-element.1024, f32[1,512,576]{1,0,2:T(1,128)S(1)} %copy.126, s32[]{:T(128)} %get-tuple-element.1020, s32[]{:T(128)} %constant.90.clone.1..sunk.1, s32[]{:T(128)} %constant.90.clone.1..sunk.1) | dynamic-update-slice | bytes 2359300 | tf_op jit(solution)/shard_map/while/body/jit(dynamic_update_index_in_dim)/dynamic_update_slice | solution.py:183
  636.4 24.3 %dynamic_update_slice.14 = f32[16,512,576]{1,0,2:T(8,128)} dynamic-update-slice(f32[16,512,576]{1,0,2:T(8,128)} %get-tuple-element.1024, f32[1,512,576]{1,0,2:T(1,128)S(1)} %copy.126, s32[]{:T(128)} %get-tuple-element.1020, s32[]{:T(128)} %constant.90.clone.1..sunk.1, s32[]{:T(128)} %constant.90.clone.1..sunk.1) | dynamic-update-slice | bytes 2359300 | tf_op jit(solution)/shard_map/while/body/jit(dynamic_update_index_in_dim)/dynamic_update_slice | solution.py:183
  665.5 24.3 %dynamic_update_slice.14 = f32[16,512,576]{1,0,2:T(8,128)} dynamic-update-slice(f32[16,512,576]{1,0,2:T(8,128)} %get-tuple-element.1024, f32[1,512,576]{1,0,2:T(1,128)S(1)} %copy.126, s32[]{:T(128)} %get-tuple-element.1020, s32[]{:T(128)} %constant.90.clone.1..sunk.1, s32[]{:T(128)} %constant.90.clone.1..sunk.1) | dynamic-update-slice | bytes 2359300 | tf_op jit(solution)/shard_map/while/body/jit(dynamic_update_index_in_dim)/dynamic_update_slice | solution.py:183
  694.6 24.3 %dynamic_update_slice.14 = f32[16,512,576]{1,0,2:T(8,128)} dynamic-update-slice(f32[16,512,576]{1,0,2:T(8,128)} %get-tuple-element.1024, f32[1,512,576]{1,0,2:T(1,128)S(1)} %copy.126, s32[]{:T(128)} %get-tuple-element.1020, s32[]{:T(128)} %constant.90.clone.1..sunk.1, s32[]{:T(128)} %constant.90.clone.1..sunk.1) | dynamic-update-slice | bytes 2359300 | tf_op jit(solution)/shard_map/while/body/jit(dynamic_update_index_in_dim)/dynamic_update_slice | solution.py:183
  723.7 24.3 %dynamic_update_slice.14 = f32[16,512,576]{1,0,2:T(8,128)} dynamic-update-slice(f32[16,512,576]{1,0,2:T(8,128)} %get-tuple-element.1024, f32[1,512,576]{1,0,2:T(1,128)S(1)} %copy.126, s32[]{:T(128)} %get-tuple-element.1020, s32[]{:T(128)} %constant.90.clone.1..sunk.1, s32[]{:T(128)} %constant.90.clone.1..sunk.1) | dynamic-update-slice | bytes 2359300 | tf_op jit(solution)/shard_map/while/body/jit(dynamic_update_index_in_dim)/dynamic_update_slice | solution.py:183
  752.9 24.3 %dynamic_update_slice.14 = f32[16,512,576]{1,0,2:T(8,128)} dynamic-update-slice(f32[16,512,576]{1,0,2:T(8,128)} %get-tuple-element.1024, f32[1,512,576]{1,0,2:T(1,128)S(1)} %copy.126, s32[]{:T(128)} %get-tuple-element.1020, s32[]{:T(128)} %constant.90.clone.1..sunk.1, s32[]{:T(128)} %constant.90.clone.1..sunk.1) | dynamic-update-slice | bytes 2359300 | tf_op jit(solution)/shard_map/while/body/jit(dynamic_update_index_in_dim)/dynamic_update_slice | solution.py:183
  777.1 19.5 %reshape_reshape.3 = f32[64,128,576]{1,0,2:T(8,128)} reshape(f32[16,512,576]{1,0,2:T(8,128)} %get-tuple-element.344) | data formatting | bytes 37748736 | tf_op jit(solution)/shard_map/reshape;reshape | solution.py:193
  796.7 17.6 %copy.100 = f32[64,128,576]{1,2,0:T(8,128)} copy(f32[64,128,576]{1,0,2:T(8,128)} %reshape_reshape.3) | data formatting | bytes 37748736 | tf_op jit(solution)/shard_map/reshape;reshape | solution.py:193
  814.3 16.1 gather_fusion.1
  830.4 14.7 broadcast_select_fusion
  845.1 20.5 %copy.101 = f32[64,128,576]{2,1,0:T(8,128)} copy(f32[64,128,576]{1,2,0:T(8,128)} %broadcast_select_fusion) | data formatting | bytes 37748736 | tf_op jit(solution)/shard_map/jit(_take)/select_n | solution.py:193
  865.5 22.5 %select_n.81 = f32[4096,1152]{1,0:T(8,128)} reshape(f32[64,128,576]{2,1,0:T(8,128)} %copy.101) | data formatting | bytes 37748736 | tf_op jit(solution)/shard_map/jit(_take)/select_n | solution.py:193
  888.1 467.7 %reduce-scatter.3.cloned.1.call-done = f32[64,1152]{1,0:T(8,128)} async-done(((f32[4096,1152]{1,0:T(8,128)}), f32[64,1152]{1,0:T(8,128)}) %reduce-scatter.3.cloned.1.call-update) | async-done | bytes 294928 | tf_op jit(solution)/shard_map/reduce_scatter | solution.py:195
  1355.8 1.8 reshape.114
  1359.2 47.3 %all-reduce.2.cloned.1.call-done = f32[128,576]{1,0:T(8,128)} async-done(((f32[128,576]{1,0:T(8,128)}), f32[128,576]{1,0:T(8,128)}) %all-reduce.2.cloned.1.call-update) | async-done | bytes 294928 | tf_op jit(solution)/shard_map/psum | solution.py:196
  1408.0 1.7 slice.50
  1409.7 288.4 %reduce-scatter.5.cloned.1.call-done = f32[8,1024]{1,0:T(8,128)} async-done(((f32[512,1024]{1,0:T(8,128)}), f32[8,1024]{1,0:T(8,128)}) %reduce-scatter.5.cloned.1.call-update) | async-done | bytes 32784 | tf_op jit(solution)/shard_map/reduce_scatter | solution.py:200
  (331 shorter events, 179.7 us)
Async XLA Ops:
  7.2 121.3 %all-gather.2.cloned.1.call-start = ((), (), s32[]{:S(2)}) async-start(), calls=%async_computation.2 | async-start | bytes 9584640 | tf_op jit(solution)/shard_map/all_gather | solution.py:51
  9.8 1346.0 %reduce-scatter.3.cloned.1.call-start = ((), (), s32[]{:S(2)}) async-start(), calls=%async_computation.3 | async-start | bytes 19169280 | tf_op jit(solution)/shard_map/reduce_scatter | solution.py:195
  168.0 7.4 slice-start
  303.8 4.8 copy-start
  888.1 518.4 %all-reduce.2.cloned.1.call-start = ((), (), s32[]{:S(2)}) async-start(), calls=%async_computation.4 | async-start | bytes 655360 | tf_op jit(solution)/shard_map/psum | solution.py:196
  1357.6 340.4 %reduce-scatter.5.cloned.1.call-start = ((), (), s32[]{:S(2)}) async-start(), calls=%async_computation.5 | async-start | bytes 2129920 | tf_op jit(solution)/shard_map/reduce_scatter | solution.py:200
Sparse Core Ops, SparseCore 0:
  10.4 117.9 all-gather.1
  888.2 467.5 reduce-scatter.2
  1358.5 47.9 all-reduce.1
  1409.4 288.6 reduce-scatter.4
where the time goes:
time: 1720 us; the launch traced here: 1700 us
  waiting for transfers between devices  913 us (53%)
  local copies, waits for them, and re-layouts  639 us (37%)
  other arithmetic  78.5 us (5%)
  loops' own time  44.8 us (3%)
    reduce_scatter x1, waiting for transfers between devices, local(): lax.psum_scatter(slot_terms, 'ctx', scatter_dimension=0, tiled=True)  468 us
    dynamic_update_slice x32, local copies, waits for them, and re-layouts, local(): lax.scan(grad_step, start_grads, (jnp.arange(step_count), kv_steps))  408 us
    reduce_scatter x1, waiting for transfers between devices, local(): lax.psum_scatter(weight_grad, 'ctx', scatter_dimension=0, tiled=True)  288 us
    all_gather x1, waiting for transfers between devices, local(): gathered = lax.all_gather(packed, 'ctx', axis=0, tiled=True)  109 us
    psum x1, waiting for transfers between devices, local(): own_rows = lax.psum(shard_sum, 'head')  47.3 us
    select_n x2, local copies, waits for them, and re-layouts, local(): jnp.take(term_rows.reshape(block_count, BLK, feat_width), block_order, ax...  43 us
    dynamic_update_slice x32, local copies, waits for them, and re-layouts, local(): lax.scan(stats_step, start_state, jnp.arange(step_count))  41 us
    another operation x2, local copies, waits for them, and re-layouts, local(): term_rows.reshape(block_count, BLK, feat_width)  37.1 us
  transfers between devices with their start and end apart: 4, of which 4 were waited for; matrix products, arithmetic and copies ran while one was open for 1% of the time, Pallas kernels for 0%

commit v1 on v0

v1 whole, which is shorter than its diff:
```python
import functools
import math

import jax
import jax.numpy as jnp
from jax import lax
from jax.experimental import pallas as pl
from jax.experimental.pallas import tpu as pltpu
from jax.sharding import PartitionSpec as P

LAT = 512
ROPE = 64
NOPE = 128
VDIM = 128
BLK = 128
HEAD = NOPE + ROPE
HALF = BLK // 2
GRP = 4
KEYS = GRP * BLK
ROWS = 2 * BLK + HALF
MOST = 36
SCALE = HEAD**-0.5
LOG2E = math.log2(math.e)
NEG = -1e30
MESH = pl.DeviceIdType.MESH
F32 = jnp.float32
BF16 = jnp.bfloat16


def nt(a, b):
    return lax.dot_general(a, b, (((1,), (1,)), ((), ())), preferred_element_type=F32)


def tn(a, b):
    return lax.dot_general(a, b, (((0,), (0,)), ((), ())), preferred_element_type=F32)


def nn(a, b):
    return jnp.dot(a, b, preferred_element_type=F32)


def pack_halves(rows):
    return jnp.concatenate([rows[:HALF], rows[HALF:]], axis=1)


def unpack_halves(rows):
    return jnp.concatenate([rows[:, :ROPE], rows[:, ROPE:]], axis=0)


def kernel(
    groups,
    zs,
    query,
    latent,
    k_rope,
    d_out,
    w_kv,
    doc,
    order,
    dq_out,
    dlat_out,
    drope_out,
    dw_out,
    kv_stage,
    q_stage,
    kv_buf,
    q_buf,
    lat_buf,
    q_lo,
    q_hi,
    g_out,
    p_buf,
    dp_buf,
    m_ref,
    mass_ref,
    ws_ref,
    fac_ref,
    delta_ref,
    dqn,
    dqr,
    t_send,
    t_recv,
    own_grad,
    kvg,
    kvt,
    dw_send,
    dw_recv,
    dw_sum,
    dw_fin,
    dq_send,
    dq_recv,
    z_send,
    z_recv,
    z_fin,
    s_kv,
    r_kv,
    s_q,
    r_q,
    s_lat,
    r_lat,
    s_blk,
    r_blk,
    s_term,
    r_term,
    s_t,
    r_t,
    s_dw,
    r_dw,
    s_dwf,
    r_dwf,
    s_dq,
    r_dq,
    s_z,
    r_z,
    s_zf,
    r_zf,
):
    ctx = lax.axis_index("ctx")
    hz = lax.axis_index("head")
    g = ctx // GRP
    j = ctx % GRP
    window = min(groups - 1, (MOST + GRP - 2) // GRP)
    w_rows = LAT // groups
    o_rows = w_rows // GRP
    z_rows = BLK // zs
    zp_rows = HALF // zs

    def mate(i):
        return ((g * GRP + (j + i) % GRP), hz)

    def other(i):
        return (((g + i) % groups) * GRP + j, hz)

    def deep(i):
        return (ctx, (hz + i) % zs)

    def remote(src, dst, send, recv, to):
        return pltpu.make_async_remote_copy(
            src_ref=src, dst_ref=dst, send_sem=send, recv_sem=recv, device_id=to, device_id_type=MESH
        )

    barrier = pltpu.get_barrier_semaphore()
    for i in range(1, GRP):
        pl.semaphore_signal(barrier, inc=1, device_id=mate(i), device_id_type=MESH)
    for i in range(1, zs):
        pl.semaphore_signal(barrier, inc=1, device_id=deep(i), device_id_type=MESH)

    def greet(i, carry):
        pl.semaphore_signal(barrier, inc=1, device_id=other(i), device_id_type=MESH)
        return carry

    lax.fori_loop(1, groups, greet, 0)

    kv = nn(latent[...], w_kv[...]).astype(BF16)
    rope_pack = pack_halves(k_rope[...])
    for h in range(GRP):
        kv_stage[h, :BLK] = kv[:, 256 * h : 256 * h + 128]
        kv_stage[h, BLK : 2 * BLK] = kv[:, 256 * h + 128 : 256 * h + 256]
        kv_stage[h, 2 * BLK :] = rope_pack
        q_stage[h, :BLK] = query[:, HEAD * h : HEAD * h + NOPE]
        q_stage[h, BLK : 2 * BLK] = d_out[:, VDIM * h : VDIM * h + VDIM]
        q_stage[h, 2 * BLK :] = pack_halves(query[:, HEAD * h + NOPE : HEAD * h + HEAD])
    lat_buf[j] = latent[...].astype(F32).T.astype(BF16)

    pl.semaphore_wait(barrier, GRP - 1 + zs - 1 + groups - 1)

    def kv_copy(i):
        return remote(kv_stage.at[(j + i) % GRP], kv_buf.at[0, j], s_kv.at[i], r_kv.at[i], mate(i))

    def q_copy(i):
        return remote(q_stage.at[(j + i) % GRP], q_buf.at[j], s_q.at[i], r_q.at[i], mate(i))

    def lat_copy(i):
        return remote(lat_buf.at[j], lat_buf.at[j], s_lat.at[i], r_lat.at[i], mate(i))

    for i in range(1, GRP):
        kv_copy(i).start()
    for i in range(1, GRP):
        q_copy(i).start()
    kv_buf[0, j] = kv_stage[j]
    q_buf[j] = q_stage[j]
    for i in range(1, GRP):
        came = kv_buf.at[0, (j + GRP - i) % GRP]
        remote(came, came, s_kv.at[i], r_kv.at[i], mate(i)).wait_recv()

    def blk_copy(d):
        return remote(kv_buf.at[0], kv_buf.at[d], s_blk.at[d], r_blk.at[d], other(d))

    def send_blk(d, carry):
        @pl.when(g + d < groups)
        def _():
            blk_copy(d).start()

        return carry

    lax.fori_loop(1, window + 1, send_blk, 0)
    for i in range(1, GRP):
        lat_copy(i).start()

    slot_of = lax.broadcasted_iota(jnp.int32, (1, KEYS), 1) // BLK
    in_slot = lax.broadcasted_iota(jnp.int32, (1, KEYS), 1) % BLK
    q_pos = jnp.zeros((1, KEYS), jnp.int32)
    q_doc = jnp.zeros((1, KEYS), jnp.int32)
    for s in range(GRP):
        block = order[GRP * g + s]
        q_pos = jnp.where(slot_of == s, block * BLK + in_slot, q_pos)
        q_doc = jnp.where(slot_of == s, doc[block], q_doc)

    m_ref[...] = jnp.full(m_ref.shape, NEG, F32)
    mass_ref[...] = jnp.zeros(mass_ref.shape, F32)
    ws_ref[...] = jnp.zeros(ws_ref.shape, F32)

    for i in range(1, GRP):
        came = q_buf.at[(j + GRP - i) % GRP]
        remote(came, came, s_q.at[i], r_q.at[i], mate(i)).wait_recv()
    blank = jnp.zeros((HALF, ROPE), BF16)
    for s in range(GRP):
        at = s * BLK
        pair = q_buf[s, 2 * BLK :]
        first, second = pair[:, :ROPE], pair[:, ROPE:]
        q_lo[at : at + BLK, :NOPE] = q_buf[s, :BLK]
        q_hi[at : at + BLK, :NOPE] = q_buf[s, :BLK]
        g_out[at : at + BLK] = q_buf[s, BLK : 2 * BLK]
        q_lo[at : at + HALF, NOPE:] = jnp.concatenate([first, blank], axis=1)
        q_lo[at + HALF : at + BLK, NOPE:] = jnp.concatenate([second, blank], axis=1)
        q_hi[at : at + HALF, NOPE:] = jnp.concatenate([blank, first], axis=1)
        q_hi[at + HALF : at + BLK, NOPE:] = jnp.concatenate([blank, second], axis=1)

    def gather_rows(d, low):
        return jnp.concatenate([kv_buf[d, s, low : low + HALF] for s in range(GRP)], axis=0)

    def keys_of(d, half):
        return jnp.concatenate([gather_rows(d, half * HALF), gather_rows(d, 2 * BLK)], axis=1)

    def scores_tile(d, local):
        top = jnp.full((8, KEYS), NEG, F32)
        for half in range(2):
            scores = nt(keys_of(d, half), (q_lo, q_hi)[half][...])
            for s in range(GRP):
                block = order[GRP * (g - d) + s]
                same = q_doc == doc[block]
                part = scores[s * HALF : s * HALF + HALF] * (SCALE * LOG2E)
                if local:
                    pos = lax.broadcasted_iota(jnp.int32, (HALF, 1), 0) + (block * BLK + half * HALF)
                    part = jnp.where(same & (pos <= q_pos), part, NEG)
                else:
                    part = part + jnp.where(same, 0.0, NEG)
                p_buf[d, half, s] = part
                top = jnp.maximum(top, jnp.max(part.reshape(HALF // 8, 8, KEYS), axis=0))
        peak = jnp.max(top, axis=0, keepdims=True)
        mass = jnp.zeros((8, KEYS), F32)
        weighted = jnp.zeros((8, KEYS), F32)
        for half in range(2):
            dp = nt(gather_rows(d, BLK + half * HALF), g_out[...])
            for s in range(GRP):
                here = dp[s * HALF : s * HALF + HALF]
                p = jnp.exp2(p_buf[d, half, s] - peak)
                p_buf[d, half, s] = p
                dp_buf[d, half, s] = here
                mass = mass + jnp.sum(p.reshape(HALF // 8, 8, KEYS), axis=0)
                weighted = weighted + jnp.sum((p * here).reshape(HALF // 8, 8, KEYS), axis=0)
        m_ref[d] = peak
        mass_ref[d] = jnp.sum(mass, axis=0, keepdims=True)
        ws_ref[d] = jnp.sum(weighted, axis=0, keepdims=True)

    scores_tile(0, True)

    def far_scores(d, carry):
        @pl.when(g >= d)
        def _():
            came = kv_buf.at[d]
            remote(came, came, s_blk.at[d], r_blk.at[d], other(d)).wait_recv()
            scores_tile(d, False)

        return carry

    lax.fori_loop(1, window + 1, far_scores, 0)

    peak = jnp.max(m_ref[...], axis=0)
    factors = jnp.exp2(m_ref[...] - peak[None])
    mass = jnp.sum(mass_ref[...] * factors, axis=0)
    weighted = jnp.sum(ws_ref[...] * factors, axis=0)
    fac_ref[...] = factors / mass[None]
    delta_ref[...] = weighted / mass
    dqn[...] = jnp.zeros(dqn.shape, F32)
    dqr[...] = jnp.zeros(dqr.shape, F32)

    def grads_tile(d, put):
        factor = fac_ref[d]
        delta = delta_ref[...]
        rope_sum = None
        for half in range(2):
            mixed, probs = [], []
            for s in range(GRP):
                p = p_buf[d, half, s] * factor
                mixed.append((p * (dp_buf[d, half, s] - delta)).astype(BF16))
                probs.append(p.astype(BF16))
            mixed = jnp.concatenate(mixed, axis=0)
            probs = jnp.concatenate(probs, axis=0)
            d_keys = nn(mixed, (q_lo, q_hi)[half][...]) * SCALE
            d_values = nn(probs, g_out[...])
            rope_sum = d_keys[:, NOPE:] if half == 0 else rope_sum + d_keys[:, NOPE:]
            for s in range(GRP):
                put(s, half * HALF, d_keys[s * HALF : s * HALF + HALF, :NOPE])
                put(s, BLK + half * HALF, d_values[s * HALF : s * HALF + HALF])
            dq = tn(keys_of(d, half), mixed)
            dqn[...] += dq[:NOPE]
            dqr[...] += dq[NOPE + half * ROPE : NOPE + half * ROPE + ROPE]
        for s in range(GRP):
            put(s, 2 * BLK, rope_sum[s * HALF : s * HALF + HALF])

    def term_copy(d):
        return remote(t_send.at[d], t_recv.at[d], s_term.at[d], r_term.at[d], other(groups - d))

    def far_grads(step, carry):
        d = window - step

        @pl.when(g >= d)
        def _():
            def put(s, low, rows):
                t_send[d, s, low : low + HALF] = rows.astype(BF16)

            grads_tile(d, put)
            term_copy(d).start()

        return carry

    lax.fori_loop(0, window, far_grads, 0)

    def put_own(s, low, rows):
        own_grad[s, low : low + HALF] = rows

    grads_tile(0, put_own)

    dq_nope = (dqn[...] * SCALE).T.astype(BF16)
    dq_rope = (dqr[...] * SCALE).T.astype(BF16)
    for s in range(GRP):
        dq_send[s, :BLK] = dq_nope[s * BLK : s * BLK + BLK]
        dq_send[s, BLK:] = pack_halves(dq_rope[s * BLK : s * BLK + BLK])
    dq_recv[j] = dq_send[j]

    def dq_copy(i):
        return remote(dq_send.at[(j + i) % GRP], dq_recv.at[j], s_dq.at[i], r_dq.at[i], mate(i))

    for i in range(1, GRP):
        dq_copy(i).start()

    def take_terms(d, carry):
        @pl.when(g + d < groups)
        def _():
            came = t_recv.at[d]
            remote(came, came, s_term.at[d], r_term.at[d], other(d)).wait_recv()
            own_grad[...] += t_recv[d].astype(F32)

        return carry

    lax.fori_loop(1, window + 1, take_terms, 0)
    kvg[...] = own_grad[...].astype(BF16)
    kvt[j] = kvg[j]

    def t_copy(i):
        return remote(kvg.at[(j + i) % GRP], kvt.at[j], s_t.at[i], r_t.at[i], mate(i))

    for i in range(1, GRP):
        t_copy(i).start()

    for i in range(1, GRP):
        came = lat_buf.at[(j + GRP - i) % GRP]
        remote(came, came, s_lat.at[i], r_lat.at[i], mate(i)).wait_recv()
    grad_w = jnp.zeros((LAT, NOPE + VDIM), F32)
    for s in range(GRP):
        pair = jnp.concatenate([kvg[s, :BLK], kvg[s, BLK : 2 * BLK]], axis=1)
        grad_w = grad_w + nn(lat_buf[s], pair)
    grad_w = grad_w.astype(BF16)
    for i in range(groups):
        dw_send[i] = grad_w[i * w_rows : (i + 1) * w_rows]

    def dw_copy(i):
        return remote(dw_send.at[(g + i) % groups], dw_recv.at[i], s_dw.at[i], r_dw.at[i], other(i))

    def send_dw(i, carry):
        dw_copy(i).start()
        return carry

    lax.fori_loop(1, groups, send_dw, 0)

    for i in range(1, GRP):
        came = kvt.at[(j + GRP - i) % GRP]
        remote(came, came, s_t.at[i], r_t.at[i], mate(i)).wait_recv()
    pairs = jnp.concatenate(
        [kvt[h, low : low + BLK] for h in range(GRP) for low in (0, BLK)], axis=1
    )
    d_lat = nt(pairs, w_kv[...])
    d_rope = kvt[0, 2 * BLK :].astype(F32)
    for h in range(1, GRP):
        d_rope = d_rope + kvt[h, 2 * BLK :].astype(F32)
    for t in range(zs):
        z_send[t, :, :LAT] = d_lat[t * z_rows : (t + 1) * z_rows].astype(BF16)
        z_send[t, :zp_rows, LAT:] = d_rope[t * zp_rows : (t + 1) * zp_rows].astype(BF16)
        z_send[t, zp_rows:, LAT:] = jnp.zeros((z_rows - zp_rows, 2 * ROPE), BF16)

    def z_copy(i):
        return remote(z_send.at[(hz + i) % zs], z_recv.at[i], s_z.at[i], r_z.at[i], deep(i))

    for i in range(1, zs):
        z_copy(i).start()

    for i in range(1, GRP):
        came = dq_recv.at[(j + GRP - i) % GRP]
        remote(came, came, s_dq.at[i], r_dq.at[i], mate(i)).wait_recv()
    columns = []
    for h in range(GRP):
        columns += [dq_recv[h, :BLK], unpack_halves(dq_recv[h, BLK:])]
    dq_out[...] = jnp.concatenate(columns, axis=1)

    z_sum = z_send[hz].astype(F32)
    for i in range(1, zs):
        remote(z_recv.at[i], z_recv.at[i], s_z.at[i], r_z.at[i], deep(i)).wait_recv()
        z_sum = z_sum + z_recv[i].astype(F32)
    z_fin[hz] = z_sum.astype(BF16)

    def zf_copy(i):
        return remote(z_fin.at[hz], z_fin.at[hz], s_zf.at[i], r_zf.at[i], deep(i))

    for i in range(1, zs):
        zf_copy(i).start()

    dw_sum[...] = dw_send[g].astype(F32)

    def take_dw(i, carry):
        remote(dw_recv.at[i], dw_recv.at[i], s_dw.at[i], r_dw.at[i], other(i)).wait_recv()
        dw_sum[...] += dw_recv[i].astype(F32)
        return carry

    lax.fori_loop(1, groups, take_dw, 0)

    def dwf_copy(i):
        rows = pl.ds(pl.multiple_of((j + i) % GRP * o_rows, o_rows), o_rows)
        return remote(dw_sum.at[rows], dw_fin.at[j], s_dwf.at[i], r_dwf.at[i], mate(i))

    for i in range(1, GRP):
        dwf_copy(i).start()
    dw_fin[j] = dw_sum[pl.ds(pl.multiple_of(j * o_rows, o_rows), o_rows)]

    for i in range(1, zs):
        came = z_fin.at[(hz + zs - i) % zs]
        remote(came, came, s_zf.at[i], r_zf.at[i], deep(i)).wait_recv()
    packed = []
    for t in range(zs):
        dlat_out[t * z_rows : (t + 1) * z_rows] = z_fin[t, :, :LAT].astype(F32)
        packed.append(z_fin[t, :zp_rows, LAT:].astype(F32))
    drope_out[...] = unpack_halves(jnp.concatenate(packed, axis=0))

    for i in range(1, GRP):
        came = dw_fin.at[(j + GRP - i) % GRP]
        remote(came, came, s_dwf.at[i], r_dwf.at[i], mate(i)).wait_recv()
    dw_out[...] = jnp.concatenate([dw_fin[h] for h in range(GRP)], axis=1)

    for i in range(1, GRP):
        kv_copy(i).wait_send()
        q_copy(i).wait_send()
        lat_copy(i).wait_send()
        dq_copy(i).wait_send()
        t_copy(i).wait_send()
        dwf_copy(i).wait_send()
    for i in range(1, zs):
        z_copy(i).wait_send()
        zf_copy(i).wait_send()

    def end_far(d, carry):
        @pl.when(g + d < groups)
        def _():
            blk_copy(d).wait_send()

        @pl.when(g >= d)
        def _():
            term_copy(d).wait_send()

        return carry

    lax.fori_loop(1, window + 1, end_far, 0)

    def end_dw(i, carry):
        dw_copy(i).wait_send()
        return carry

    lax.fori_loop(1, groups, end_dw, 0)


def solution(mesh):
    groups = mesh.shape["ctx"] // GRP
    zs = mesh.shape["head"]
    span = min(groups - 1, (MOST + GRP - 2) // GRP) + 1
    w_rows = LAT // groups
    z_rows = BLK // zs
    vmem = pltpu.VMEM
    dma = pltpu.SemaphoreType.DMA
    scratch = [
        vmem((GRP, ROWS, 128), BF16),
        vmem((GRP, ROWS, 128), BF16),
        vmem((span, GRP, ROWS, 128), BF16),
        vmem((GRP, ROWS, 128), BF16),
        vmem((GRP, LAT, BLK), BF16),
        vmem((KEYS, 256), BF16),
        vmem((KEYS, 256), BF16),
        vmem((KEYS, VDIM), BF16),
        vmem((span, 2, GRP, HALF, KEYS), F32),
        vmem((span, 2, GRP, HALF, KEYS), F32),
        vmem((span, 1, KEYS), F32),
        vmem((span, 1, KEYS), F32),
        vmem((span, 1, KEYS), F32),
        vmem((span, 1, KEYS), F32),
        vmem((1, KEYS), F32),
        vmem((NOPE, KEYS), F32),
        vmem((ROPE, KEYS), F32),
        vmem((span, GRP, ROWS, 128), BF16),
        vmem((span, GRP, ROWS, 128), BF16),
        vmem((GRP, ROWS, 128), F32),
        vmem((GRP, ROWS, 128), BF16),
        vmem((GRP, ROWS, 128), BF16),
        vmem((groups, w_rows, 256), BF16),
        vmem((groups, w_rows, 256), BF16),
        vmem((w_rows, 256), F32),
        vmem((GRP, w_rows // GRP, 256), F32),
        vmem((GRP, BLK + HALF, 128), BF16),
        vmem((GRP, BLK + HALF, 128), BF16),
        vmem((zs, z_rows, LAT + 128), BF16),
        vmem((zs, z_rows, LAT + 128), BF16),
        vmem((zs, z_rows, LAT + 128), BF16),
    ]
    for count in (GRP, GRP, GRP, span, span, GRP, groups, GRP, GRP, zs, zs):
        scratch += [dma((count,)), dma((count,))]

    def local(query, latent, k_rope, d_out, w_kv, block_doc, block_order):
        whole = pl.BlockSpec(memory_space=pltpu.VMEM)
        scalars = pl.BlockSpec(memory_space=pltpu.SMEM)
        return pl.pallas_call(
            functools.partial(kernel, groups, zs),
            out_shape=(
                jax.ShapeDtypeStruct(query.shape, BF16),
                jax.ShapeDtypeStruct((BLK, LAT), F32),
                jax.ShapeDtypeStruct((BLK, ROPE), F32),
                jax.ShapeDtypeStruct((w_rows // GRP, GRP * 256), F32),
            ),
            in_specs=[whole] * 5 + [scalars] * 2,
            out_specs=(whole,) * 4,
            scratch_shapes=scratch,
            compiler_params=pltpu.CompilerParams(
                collective_id=0, has_side_effects=True, vmem_limit_bytes=56 * 1024 * 1024
            ),
        )(query, latent, k_rope, d_out, w_kv, block_doc, block_order)

    return jax.shard_map(
        local,
        mesh=mesh,
        in_specs=(
            P("ctx", "head"),
            P("ctx", None),
            P("ctx", None),
            P("ctx", "head"),
            P(None, "head"),
            P(),
            P(),
        ),
        out_specs=(P("ctx", "head"), P("ctx", None), P("ctx", None), P("ctx", "head")),
        check_vma=False,
    )
```

time: 1720 us -> 152 us (0.09)
  the two profiles are of different devices: /device:TPU:64 before, /device:TPU:22 now
where the time goes in v1:
time: 152 us; the launch traced here: 151 us
  Pallas kernels  145 us (95%)
  local copies, waits for them, and re-layouts  6 us (4%)
    pallas_call x1, Pallas kernels, local(): pl.pallas_call(functools.partial(kernel, groups, zs), out_shape=(jax.Shap...  145 us
    unnamed x8, local copies, waits for them, and re-layouts  4.43 us

profile of v1, /device:TPU:22, one launch (start us, length us, event | category | flops | bytes accessed | tf_op | source)
XLA Modules:
  0.0 151.4 jit_solution(6911991412603596428)
XLA Ops:
  0.6 1.4 copy.11.k_rope
  2.1 144.8 %shard_map.102 = (bf16[128,768]{1,0:T(8,128)(2,1)}, f32[128,512]{1,0:T(8,128)}, f32[128,64]{1,0:T(8,128)}, f32[8,1024]{1,0:T(8,128)}) custom-call(bf16[128,768]{1,0:T(8,128)(2,1)} %query.1, bf16[128,512]{1,0:T(8,128)(2,1)} %latent.1, bf16[128,64]{1,0:T(8,128)(2,1)} %copy.11.k_rope, bf16[128,512]{1,0:T(8,128)(2,1)} %d_out.1, bf16[512,1024]{1,0:T(8,128)(2,1)} %w_kv.1, ...), custom_call_target="tpu_custom_call" | custom-call | tf_op jit(solution)/shard_map/pallas_call | solution.py:537
  146.9 0.0 copy-start
  146.9 1.6 %copy.12 = f32[128,64]{0,1:T(8,128)} copy(f32[128,64]{1,0:T(8,128)} %get-tuple-element.6) | data formatting | bytes 65536 | tf_op jit(solution)/shard_map/pallas_call | solution.py:537
  148.5 1.6 %copy.16 = bf16[128,768]{1,0:T(8,128)(2,1)} copy(bf16[128,768]{1,0:T(8,128)(2,1)} %get-tuple-element.12) | data formatting | bytes 393216
  150.1 0.0 copy-done
  150.1 0.0 copy-start.1
  150.1 0.7 copy.17
  150.8 0.1 copy-done.1
  150.8 0.6 copy.18
Async XLA Ops:
  146.9 3.2 %copy-start = (f32[128,512]{1,0:T(8,128)S(1)}, f32[128,512]{1,0:T(8,128)}, u32[]{:S(2)}) copy-start(f32[128,512]{1,0:T(8,128)} %get-tuple-element.13) | copy-start | bytes 786436
  150.1 0.8 copy-start.1

commit v2 on v1

v2 whole, which is shorter than its diff:
```python
import functools
import math

import jax
import jax.numpy as jnp
from jax import lax
from jax.experimental import pallas as pl
from jax.experimental.pallas import tpu as pltpu
from jax.sharding import PartitionSpec as P

LAT = 512
ROPE = 64
NOPE = 128
VDIM = 128
BLK = 128
HEAD = NOPE + ROPE
HALF = BLK // 2
GRP = 4
KEYS = GRP * BLK
ROWS = 2 * BLK + HALF
COLS = LAT // BLK
PIECE = LAT + HALF
MOST = 36
SCALE = HEAD**-0.5
LOG2E = math.log2(math.e)
NEG = -1e30
MESH = pl.DeviceIdType.MESH
F32 = jnp.float32
BF16 = jnp.bfloat16


def nt(a, b):
    return lax.dot_general(a, b, (((1,), (1,)), ((), ())), preferred_element_type=F32)


def tn(a, b):
    return lax.dot_general(a, b, (((0,), (0,)), ((), ())), preferred_element_type=F32)


def nn(a, b):
    return jnp.dot(a, b, preferred_element_type=F32)


def pack_halves(rows):
    return jnp.concatenate([rows[:HALF], rows[HALF:]], axis=1)


def unpack_halves(rows):
    return jnp.concatenate([rows[:, :ROPE], rows[:, ROPE:]], axis=0)


def kernel(
    groups,
    zs,
    query,
    latent,
    k_rope,
    d_out,
    w_kv,
    doc,
    order,
    dq_out,
    dlat_out,
    drope_out,
    dw_out,
    q_stage,
    q_buf,
    lat_buf,
    k_buf,
    w_head,
    q_lo,
    q_hi,
    g_out,
    p_buf,
    dp_buf,
    m_ref,
    mass_ref,
    ws_ref,
    fac_ref,
    delta_ref,
    dqn,
    dqr,
    dw_acc,
    terms,
    core_recv,
    near_send,
    near_recv,
    far_send,
    far_recv,
    total,
    dw_send,
    dw_recv,
    dw_sum,
    dw_fin,
    dq_send,
    dq_recv,
    z_send,
    z_recv,
    z_fin,
    s_q,
    r_q,
    s_far,
    r_far,
    s_own,
    r_own,
    s_near,
    r_near,
    s_pass,
    r_pass,
    s_tc,
    r_tc,
    s_tx,
    r_tx,
    s_tn,
    r_tn,
    s_tf,
    r_tf,
    s_dw,
    r_dw,
    s_dwf,
    r_dwf,
    s_dq,
    r_dq,
    s_z,
    r_z,
    s_zf,
    r_zf,
):
    ctx = lax.axis_index("ctx")
    hz = lax.axis_index("head")
    g = ctx // GRP
    j = ctx % GRP
    z_lo = j // 2
    core = j % 2
    j_core = 2 * z_lo + 1 - core
    j_near = 2 * (1 - z_lo) + core
    j_next = 2 * (1 - z_lo) + 1 - core
    window = min(groups - 1, (MOST + GRP - 2) // GRP)
    w_rows = LAT // groups
    o_rows = w_rows // GRP
    z_rows = BLK // zs
    zp_rows = HALF // zs

    def mate(i):
        return ((g * GRP + (j + i) % GRP), hz)

    def other(i):
        return (((g + i) % groups) * GRP + j, hz)

    def deep(i):
        return (ctx, (hz + i) % zs)

    beside = (g * GRP + j_core, hz)
    ahead = (g * GRP + j_near, (hz + z_lo + core * (zs - 1)) % zs)
    behind = (g * GRP + j_near, (hz + z_lo + (1 - core) * (zs - 1)) % zs)

    def remote(src, dst, send, recv, to):
        return pltpu.make_async_remote_copy(
            src_ref=src, dst_ref=dst, send_sem=send, recv_sem=recv, device_id=to, device_id_type=MESH
        )

    def arrived(ref, sem, to):
        remote(ref, ref, sem, sem, to).wait_recv()

    barrier = pltpu.get_barrier_semaphore()
    for i in range(1, GRP):
        pl.semaphore_signal(barrier, inc=1, device_id=mate(i), device_id_type=MESH)
    for i in range(1, zs):
        pl.semaphore_signal(barrier, inc=1, device_id=deep(i), device_id_type=MESH)
    pl.semaphore_signal(barrier, inc=1, device_id=ahead, device_id_type=MESH)
    pl.semaphore_signal(barrier, inc=1, device_id=behind, device_id_type=MESH)

    def greet(i, carry):
        pl.semaphore_signal(barrier, inc=1, device_id=other(i), device_id_type=MESH)
        return carry

    lax.fori_loop(1, groups, greet, 0)

    for c in range(COLS):
        lat_buf[0, j, c * BLK : (c + 1) * BLK] = latent[:, c * BLK : (c + 1) * BLK]
    lat_buf[0, j, LAT:] = pack_halves(k_rope[...].astype(F32).T.astype(BF16))
    for h in range(GRP):
        q_stage[h, :BLK] = query[:, HEAD * h : HEAD * h + NOPE]
        q_stage[h, BLK : 2 * BLK] = d_out[:, VDIM * h : VDIM * h + VDIM]
        q_stage[h, 2 * BLK :] = pack_halves(query[:, HEAD * h + NOPE : HEAD * h + HEAD])

    pl.semaphore_wait(barrier, GRP - 1 + zs - 1 + 2 + groups - 1)

    def far_copy(d):
        return remote(lat_buf.at[0, j], lat_buf.at[d, j], s_far.at[d], r_far.at[d], other(d))

    def own_copy(d):
        return remote(lat_buf.at[d, j], lat_buf.at[d, j], s_own.at[d], r_own.at[d], beside)

    def near_copy(d):
        return remote(lat_buf.at[d, j], lat_buf.at[d, j], s_near.at[d], r_near.at[d], ahead)

    def pass_copy(d):
        return remote(lat_buf.at[d, j_near], lat_buf.at[d, j_near], s_pass.at[d], r_pass.at[d], beside)

    def q_copy(i):
        return remote(q_stage.at[(j + i) % GRP], q_buf.at[j], s_q.at[i], r_q.at[i], mate(i))

    def send_far(d, carry):
        @pl.when(g + d < groups)
        def _():
            far_copy(d).start()

        return carry

    near_copy(0).start()
    own_copy(0).start()
    lax.fori_loop(1, window + 1, send_far, 0)
    for i in range(1, GRP):
        q_copy(i).start()
    q_buf[j] = q_stage[j]
    w_head[...] = w_kv[:, pl.ds(pl.multiple_of(j * 256, 256), 256)]

    slot_of = lax.broadcasted_iota(jnp.int32, (1, KEYS), 1) // BLK
    in_slot = lax.broadcasted_iota(jnp.int32, (1, KEYS), 1) % BLK
    q_pos = jnp.zeros((1, KEYS), jnp.int32)
    q_doc = jnp.zeros((1, KEYS), jnp.int32)
    for s in range(GRP):
        block = order[GRP * g + s]
        q_pos = jnp.where(slot_of == s, block * BLK + in_slot, q_pos)
        q_doc = jnp.where(slot_of == s, doc[block], q_doc)

    m_ref[...] = jnp.full(m_ref.shape, NEG, F32)
    mass_ref[...] = jnp.zeros(mass_ref.shape, F32)
    ws_ref[...] = jnp.zeros(ws_ref.shape, F32)

    def latents_of(d):
        return jnp.concatenate(
            [
                jnp.concatenate([lat_buf[d, s, c * BLK : (c + 1) * BLK] for c in range(COLS)], axis=1)
                for s in range(GRP)
            ],
            axis=0,
        )

    def half_rows(rows, half):
        return jnp.concatenate(
            [rows[s * BLK + half * HALF : s * BLK + half * HALF + HALF] for s in range(GRP)], axis=0
        )

    def scores_tile(d, local):
        kv = nn(latents_of(d), w_head[...]).astype(BF16)
        rope = jnp.concatenate([lat_buf[d, s, LAT:] for s in range(GRP)], axis=0)
        top = jnp.full((8, KEYS), NEG, F32)
        for half in range(2):
            k_buf[d, half] = jnp.concatenate([half_rows(kv[:, :NOPE], half), rope], axis=1)
            scores = nt(k_buf[d, half], (q_lo, q_hi)[half][...])
            for s in range(GRP):
                block = order[GRP * (g - d) + s]
                same = q_doc == doc[block]
                part = scores[s * HALF : s * HALF + HALF] * (SCALE * LOG2E)
                if local:
                    pos = lax.broadcasted_iota(jnp.int32, (HALF, 1), 0) + (block * BLK + half * HALF)
                    part = jnp.where(same & (pos <= q_pos), part, NEG)
                else:
                    part = part + jnp.where(same, 0.0, NEG)
                p_buf[d, half, s] = part
                top = jnp.maximum(top, jnp.max(part.reshape(HALF // 8, 8, KEYS), axis=0))
        peak = jnp.max(top, axis=0, keepdims=True)
        mass = jnp.zeros((8, KEYS), F32)
        weighted = jnp.zeros((8, KEYS), F32)
        for half in range(2):
            dp = nt(half_rows(kv[:, NOPE:], half), g_out[...])
            for s in range(GRP):
                here = dp[s * HALF : s * HALF + HALF]
                p = jnp.exp2(p_buf[d, half, s] - peak)
                p_buf[d, half, s] = p
                dp_buf[d, half, s] = here
                mass = mass + jnp.sum(p.reshape(HALF // 8, 8, KEYS), axis=0)
                weighted = weighted + jnp.sum((p * here).reshape(HALF // 8, 8, KEYS), axis=0)
        m_ref[d] = peak
        mass_ref[d] = jnp.sum(mass, axis=0, keepdims=True)
        ws_ref[d] = jnp.sum(weighted, axis=0, keepdims=True)

    def spread(d):
        @pl.when((d <= window) & (g >= d))
        def _():
            arrived(lat_buf.at[d, j], r_far.at[d], beside)
            near_copy(d).start()
            own_copy(d).start()

    def hand_on(d):
        @pl.when((d <= window) & (g >= d))
        def _():
            arrived(lat_buf.at[d, j_near], r_near.at[d], beside)
            pass_copy(d).start()

    def whole(d):
        arrived(lat_buf.at[d, j_core], r_own.at[d], beside)
        arrived(lat_buf.at[d, j_next], r_pass.at[d], beside)

    hand_on(0)
    for i in range(1, GRP):
        arrived(q_buf.at[(j + GRP - i) % GRP], r_q.at[i], mate(i))
    blank = jnp.zeros((HALF, ROPE), BF16)
    for s in range(GRP):
        at = s * BLK
        pair = q_buf[s, 2 * BLK :]
        first, second = pair[:, :ROPE], pair[:, ROPE:]
        q_lo[at : at + BLK, :NOPE] = q_buf[s, :BLK]
        q_hi[at : at + BLK, :NOPE] = q_buf[s, :BLK]
        g_out[at : at + BLK] = q_buf[s, BLK : 2 * BLK]
        q_lo[at : at + HALF, NOPE:] = jnp.concatenate([first, blank], axis=1)
        q_lo[at + HALF : at + BLK, NOPE:] = jnp.concatenate([second, blank], axis=1)
        q_hi[at : at + HALF, NOPE:] = jnp.concatenate([blank, first], axis=1)
        q_hi[at + HALF : at + BLK, NOPE:] = jnp.concatenate([blank, second], axis=1)
    spread(1)
    whole(0)
    scores_tile(0, True)

    def far_scores(i, carry):
        spread(i)
        hand_on(i - 1)

        @pl.when(g >= i - 2)
        def _():
            whole(i - 2)
            scores_tile(i - 2, False)

        return carry

    spread(2)
    hand_on(1)
    lax.fori_loop(3, window + 3, far_scores, 0)

    peak = jnp.max(m_ref[...], axis=0)
    factors = jnp.exp2(m_ref[...] - peak[None])
    mass = jnp.sum(mass_ref[...] * factors, axis=0)
    weighted = jnp.sum(ws_ref[...] * factors, axis=0)
    fac_ref[...] = factors / mass[None]
    delta_ref[...] = weighted / mass
    dqn[...] = jnp.zeros(dqn.shape, F32)
    dqr[...] = jnp.zeros(dqr.shape, F32)
    dw_acc[...] = jnp.zeros(dw_acc.shape, F32)

    def grads_tile(d):
        factor = fac_ref[d]
        delta = delta_ref[...]
        rope_sum = None
        pairs = []
        for half in range(2):
            mixed, probs = [], []
            for s in range(GRP):
                p = p_buf[d, half, s] * factor
                mixed.append((p * (dp_buf[d, half, s] - delta)).astype(BF16))
                probs.append(p.astype(BF16))
            mixed = jnp.concatenate(mixed, axis=0)
            probs = jnp.concatenate(probs, axis=0)
            d_keys = nn(mixed, (q_lo, q_hi)[half][...]) * SCALE
            d_values = nn(probs, g_out[...])
            rope_sum = d_keys[:, NOPE:] if half == 0 else rope_sum + d_keys[:, NOPE:]
            pairs.append(jnp.concatenate([d_keys[:, :NOPE], d_values], axis=1).astype(BF16))
            dq = tn(k_buf[d, half], mixed)
            dqn[...] += dq[:NOPE]
            dqr[...] += dq[NOPE + half * ROPE : NOPE + half * ROPE + ROPE]
        pairs = jnp.concatenate(
            [pairs[half][s * HALF : s * HALF + HALF] for s in range(GRP) for half in range(2)], axis=0
        )
        d_lat = nt(pairs, w_head[...])
        for s in range(GRP):
            for c in range(COLS):
                part = d_lat[s * BLK : (s + 1) * BLK, c * BLK : (c + 1) * BLK]
                terms[d, s, c * BLK : (c + 1) * BLK] = part.astype(BF16)
            terms[d, s, LAT:] = rope_sum[s * HALF : s * HALF + HALF].astype(BF16)
        dw_acc[...] += tn(pairs, latents_of(d))

    def tc_copy(d):
        return remote(terms.at[d, j_core], core_recv.at[d, 0], s_tc.at[d], r_tc.at[d], beside)

    def tx_copy(d):
        return remote(terms.at[d, j_next], core_recv.at[d, 1], s_tx.at[d], r_tx.at[d], beside)

    def tn_copy(d):
        return remote(near_send.at[d], near_recv.at[d], s_tn.at[d], r_tn.at[d], behind)

    def tf_copy(d):
        return remote(far_send.at[d], far_recv.at[d], s_tf.at[d], r_tf.at[d], other(groups - d))

    def chip_sum(d):
        @pl.when((d <= window) & (g >= d))
        def _():
            arrived(core_recv.at[d, 1], r_tx.at[d], beside)
            near_send[d] = (terms[d, j_near].astype(F32) + core_recv[d, 1].astype(F32)).astype(BF16)
            tn_copy(d).start()

    def slot_sum(d):
        arrived(core_recv.at[d, 0], r_tc.at[d], beside)
        arrived(near_recv.at[d], r_tn.at[d], beside)
        return terms[d, j].astype(F32) + core_recv[d, 0].astype(F32) + near_recv[d].astype(F32)

    def send_terms(d):
        @pl.when((d <= window) & (g >= d))
        def _():
            far_send[d] = slot_sum(d).astype(BF16)
            tf_copy(d).start()

    def far_grads(step, carry):
        d = window - step

        @pl.when(g >= d)
        def _():
            grads_tile(d)
            tx_copy(d).start()
            tc_copy(d).start()

        chip_sum(d + 1)
        send_terms(d + 2)
        return carry

    lax.fori_loop(0, window + 1, far_grads, 0)
    chip_sum(0)
    send_terms(1)

    dq_nope = (dqn[...] * SCALE).T.astype(BF16)
    dq_rope = (dqr[...] * SCALE).T.astype(BF16)
    for s in range(GRP):
        dq_send[s, :BLK] = dq_nope[s * BLK : s * BLK + BLK]
        dq_send[s, BLK:] = pack_halves(dq_rope[s * BLK : s * BLK + BLK])
    dq_recv[j] = dq_send[j]

    def dq_copy(i):
        return remote(dq_send.at[(j + i) % GRP], dq_recv.at[j], s_dq.at[i], r_dq.at[i], mate(i))

    for i in range(1, GRP):
        dq_copy(i).start()

    grad_w = dw_acc[...].T.astype(BF16)
    for i in range(groups):
        dw_send[i] = grad_w[i * w_rows : (i + 1) * w_rows]

    def dw_copy(i):
        return remote(dw_send.at[(g + i) % groups], dw_recv.at[i], s_dw.at[i], r_dw.at[i], other(i))

    def send_dw(i, carry):
        dw_copy(i).start()
        return carry

    lax.fori_loop(1, groups, send_dw, 0)

    total[...] = slot_sum(0)

    def take_terms(d, carry):
        @pl.when(g + d < groups)
        def _():
            arrived(far_recv.at[d], r_tf.at[d], other(d))
            total[...] += far_recv[d].astype(F32)

        return carry

    lax.fori_loop(1, window + 1, take_terms, 0)
    for t in range(zs):
        for c in range(COLS):
            z_send[t, c * z_rows : (c + 1) * z_rows] = total[
                c * BLK + t * z_rows : c * BLK + (t + 1) * z_rows
            ].astype(BF16)
        z_send[t, COLS * z_rows :] = total[LAT + t * zp_rows : LAT + (t + 1) * zp_rows].astype(BF16)

    def z_copy(i):
        return remote(z_send.at[(hz + i) % zs], z_recv.at[i], s_z.at[i], r_z.at[i], deep(i))

    for i in range(1, zs):
        z_copy(i).start()

    for i in range(1, GRP):
        arrived(dq_recv.at[(j + GRP - i) % GRP], r_dq.at[i], mate(i))
    columns = []
    for h in range(GRP):
        columns += [dq_recv[h, :BLK], unpack_halves(dq_recv[h, BLK:])]
    dq_out[...] = jnp.concatenate(columns, axis=1)

    z_sum = z_send[hz].astype(F32)
    for i in range(1, zs):
        arrived(z_recv.at[i], r_z.at[i], deep(i))
        z_sum = z_sum + z_recv[i].astype(F32)
    z_fin[hz] = z_sum.astype(BF16)

    def zf_copy(i):
        return remote(z_fin.at[hz], z_fin.at[hz], s_zf.at[i], r_zf.at[i], deep(i))

    for i in range(1, zs):
        zf_copy(i).start()

    dw_sum[...] = dw_send[g].astype(F32)

    def take_dw(i, carry):
        arrived(dw_recv.at[i], r_dw.at[i], other(i))
        dw_sum[...] += dw_recv[i].astype(F32)
        return carry

    lax.fori_loop(1, groups, take_dw, 0)

    def dwf_copy(i):
        rows = pl.ds(pl.multiple_of((j + i) % GRP * o_rows, o_rows), o_rows)
        return remote(dw_sum.at[rows], dw_fin.at[j], s_dwf.at[i], r_dwf.at[i], mate(i))

    for i in range(1, GRP):
        dwf_copy(i).start()
    dw_fin[j] = dw_sum[pl.ds(pl.multiple_of(j * o_rows, o_rows), o_rows)]

    for i in range(1, zs):
        arrived(z_fin.at[(hz + zs - i) % zs], r_zf.at[i], deep(i))
    packed = []
    for t in range(zs):
        for c in range(COLS):
            part = z_fin[t, c * z_rows : (c + 1) * z_rows].astype(F32)
            dlat_out[t * z_rows : (t + 1) * z_rows, c * BLK : (c + 1) * BLK] = part
        packed.append(z_fin[t, COLS * z_rows :].astype(F32))
    packed = jnp.concatenate(packed, axis=0).T
    drope_out[...] = jnp.concatenate([packed[:ROPE], packed[ROPE:]], axis=1)

    for i in range(1, GRP):
        arrived(dw_fin.at[(j + GRP - i) % GRP], r_dwf.at[i], mate(i))
    dw_out[...] = jnp.concatenate([dw_fin[h] for h in range(GRP)], axis=1)

    for i in range(1, GRP):
        q_copy(i).wait_send()
        dq_copy(i).wait_send()
        dwf_copy(i).wait_send()
    for i in range(1, zs):
        z_copy(i).wait_send()
        zf_copy(i).wait_send()

    def end_blocks(d, carry):
        @pl.when((d > 0) & (g + d < groups))
        def _():
            far_copy(d).wait_send()

        @pl.when(g >= d)
        def _():
            own_copy(d).wait_send()
            near_copy(d).wait_send()
            pass_copy(d).wait_send()
            tc_copy(d).wait_send()
            tx_copy(d).wait_send()
            tn_copy(d).wait_send()

        @pl.when((d > 0) & (g >= d))
        def _():
            tf_copy(d).wait_send()

        return carry

    lax.fori_loop(0, window + 1, end_blocks, 0)

    def end_dw(i, carry):
        dw_copy(i).wait_send()
        return carry

    lax.fori_loop(1, groups, end_dw, 0)


def solution(mesh):
    groups = mesh.shape["ctx"] // GRP
    zs = mesh.shape["head"]
    span = min(groups - 1, (MOST + GRP - 2) // GRP) + 1
    w_rows = LAT // groups
    z_piece = PIECE // zs
    vmem = pltpu.VMEM
    dma = pltpu.SemaphoreType.DMA
    scratch = [
        vmem((GRP, ROWS, 128), BF16),
        vmem((GRP, ROWS, 128), BF16),
        vmem((span, GRP, PIECE, 128), BF16),
        vmem((span, 2, KEYS // 2, 256), BF16),
        vmem((LAT, 256), BF16),
        vmem((KEYS, 256), BF16),
        vmem((KEYS, 256), BF16),
        vmem((KEYS, VDIM), BF16),
        vmem((span, 2, GRP, HALF, KEYS), F32),
        vmem((span, 2, GRP, HALF, KEYS), F32),
        vmem((span, 1, KEYS), F32),
        vmem((span, 1, KEYS), F32),
        vmem((span, 1, KEYS), F32),
        vmem((span, 1, KEYS), F32),
        vmem((1, KEYS), F32),
        vmem((NOPE, KEYS), F32),
        vmem((ROPE, KEYS), F32),
        vmem((256, LAT), F32),
        vmem((span, GRP, PIECE, 128), BF16),
        vmem((span, 2, PIECE, 128), BF16),
        vmem((span, PIECE, 128), BF16),
        vmem((span, PIECE, 128), BF16),
        vmem((span, PIECE, 128), BF16),
        vmem((span, PIECE, 128), BF16),
        vmem((PIECE, 128), F32),
        vmem((groups, w_rows, 256), BF16),
        vmem((groups, w_rows, 256), BF16),
        vmem((w_rows, 256), F32),
        vmem((GRP, w_rows // GRP, 256), F32),
        vmem((GRP, BLK + HALF, 128), BF16),
        vmem((GRP, BLK + HALF, 128), BF16),
        vmem((zs, z_piece, 128), BF16),
        vmem((zs, z_piece, 128), BF16),
        vmem((zs, z_piece, 128), BF16),
    ]
    for count in (GRP, *[span] * 8, groups, GRP, GRP, zs, zs):
        scratch += [dma((count,)), dma((count,))]

    def local(query, latent, k_rope, d_out, w_kv, block_doc, block_order):
        whole = pl.BlockSpec(memory_space=pltpu.VMEM)
        scalars = pl.BlockSpec(memory_space=pltpu.SMEM)
        d_query, d_latent, d_rope, d_w_kv = pl.pallas_call(
            functools.partial(kernel, groups, zs),
            out_shape=(
                jax.ShapeDtypeStruct(query.shape, BF16),
                jax.ShapeDtypeStruct((BLK, LAT), F32),
                jax.ShapeDtypeStruct((ROPE, BLK), F32),
                jax.ShapeDtypeStruct((w_rows // GRP, GRP * 256), F32),
            ),
            in_specs=[whole] * 5 + [scalars] * 2,
            out_specs=(whole,) * 4,
            scratch_shapes=scratch,
            compiler_params=pltpu.CompilerParams(
                collective_id=0, has_side_effects=True, vmem_limit_bytes=56 * 1024 * 1024
            ),
        )(query, latent, k_rope.T, d_out, w_kv, block_doc, block_order)
        return d_query, d_latent, d_rope.T, d_w_kv

    return jax.shard_map(
        local,
        mesh=mesh,
        in_specs=(
            P("ctx", "head"),
            P("ctx", None),
            P("ctx", None),
            P("ctx", "head"),
            P(None, "head"),
            P(),
            P(),
        ),
        out_specs=(P("ctx", "head"), P("ctx", None), P("ctx", None), P("ctx", "head")),
        check_vma=False,
    )
```

time: 152 us -> 107 us (0.70)
  the two profiles are of different devices: /device:TPU:22 before, /device:TPU:16 now
where the time goes in v2:
time: 107 us; the launch traced here: 106 us
  Pallas kernels  102 us (95%)
  local copies, waits for them, and re-layouts  3.8 us (4%)
    pallas_call x1, Pallas kernels, local(): pl.pallas_call(functools.partial(kernel, groups, zs), out_shape=(jax.Shap...  102 us
    unnamed x10, local copies, waits for them, and re-layouts  3.8 us

profile of v2, /device:TPU:16, one launch (start us, length us, event | category | flops | bytes accessed | tf_op | source)
XLA Modules:
  0.0 106.4 jit_solution(1624370893862570048)
XLA Ops:
  0.6 101.9 %shard_map.102 = (bf16[128,768]{1,0:T(8,128)(2,1)}, f32[128,512]{1,0:T(8,128)}, f32[64,128]{1,0:T(8,128)}, f32[8,1024]{1,0:T(8,128)}) custom-call(bf16[128,768]{1,0:T(8,128)(2,1)} %query.1, bf16[128,512]{1,0:T(8,128)(2,1)} %latent.1, bf16[64,128]{1,0:T(8,128)(2,1)} %bitcast.3, bf16[128,512]{1,0:T(8,128)(2,1)} %d_out.1, bf16[512,1024]{1,0:T(8,128)(2,1)} %w_kv.1, ...), custom_call_target="tpu_custom_call" | custom-call | tf_op jit(solution)/shard_map/pallas_call | solution.py:607
  102.5 0.0 copy-start
  102.6 1.7 %copy.15 = bf16[128,768]{1,0:T(8,128)(2,1)} copy(bf16[128,768]{1,0:T(8,128)(2,1)} %get-tuple-element.16) | data formatting | bytes 393216
  104.2 0.0 copy-done
  104.2 0.0 copy-start.2
  104.2 0.7 copy.16
  104.9 0.1 copy-done.2
  105.0 0.0 copy-start.1
  105.0 0.6 copy.17
  105.6 0.2 copy-done.1
  105.7 0.6 copy.18
Async XLA Ops:
  102.5 1.7 %copy-start = (f32[128,512]{1,0:T(8,128)S(1)}, f32[128,512]{1,0:T(8,128)}, u32[]{:S(2)}) copy-start(f32[128,512]{1,0:T(8,128)} %get-tuple-element.17) | copy-start | bytes 786436
  104.2 0.8 copy-start.2
  105.0 0.8 copy-start.1

commit v3 on v2

--- a/solution.py
+++ b/solution.py
@@ -15,11 +15,14 @@
 BLK = 128
 HEAD = NOPE + ROPE
 HALF = BLK // 2
+SIDE = 4
 GRP = 4
 KEYS = GRP * BLK
 ROWS = 2 * BLK + HALF
 COLS = LAT // BLK
 PIECE = LAT + HALF
+PASS_LAG, TILE_LAG = 3, 5
+CHIP_LAG, SLOT_LAG = 1, 4
 MOST = 36
 SCALE = HEAD**-0.5
 LOG2E = math.log2(math.e)
@@ -87,6 +90,8 @@
     near_recv,
     far_send,
     far_recv,
+    up_send,
+    up_recv,
     total,
     dw_send,
     dw_recv,
@@ -99,7 +104,9 @@
     z_fin,
     s_q,
     r_q,
-    s_far,
+    s_down,
+    s_fan,
+    s_corner,
     r_far,
     s_own,
     r_own,
@@ -115,6 +122,8 @@
     r_tn,
     s_tf,
     r_tf,
+    s_up,
+    r_up,
     s_dw,
     r_dw,
     s_dwf,
@@ -136,6 +145,8 @@
     j_near = 2 * (1 - z_lo) + core
     j_next = 2 * (1 - z_lo) + 1 - core
     window = min(groups - 1, (MOST + GRP - 2) // GRP)
+    y = g // SIDE
+    x = g % SIDE
     w_rows = LAT // groups
     o_rows = w_rows // GRP
     z_rows = BLK // zs
@@ -186,8 +197,33 @@
 
     pl.semaphore_wait(barrier, GRP - 1 + zs - 1 + 2 + groups - 1)
 
-    def far_copy(d):
-        return remote(lat_buf.at[0, j], lat_buf.at[d, j], s_far.at[d], r_far.at[d], other(d))
+    def row_mate(i):
+        return ((g - x + (x + i) % SIDE) * GRP + j, hz)
+
+    def down_copy(dy):
+        here, there = SIDE * dy, SIDE * (dy + 1)
+        to = ((g + SIDE) * GRP + j, hz)
+        return remote(lat_buf.at[here, j], lat_buf.at[there, j], s_down.at[dy], r_far.at[there], to)
+
+    def fan_copy(dy, i):
+        d = SIDE * dy + (x + i) % SIDE - x
+        return remote(lat_buf.at[SIDE * dy, j], lat_buf.at[d, j], s_fan.at[dy, i], r_far.at[d], row_mate(i))
+
+    def in_fan(dy, i):
+        d = SIDE * dy + (x + i) % SIDE - x
+        return (y >= dy) & (d >= 1) & (d <= window)
+
+    corner_out = (y == 0) & (x == SIDE - 1)
+
+    def corner_copy():
+        return remote(lat_buf.at[0, j], lat_buf.at[window, j], s_corner.at[0], r_far.at[window], other(window))
+
+    def fan(dy):
+        for i in (1, 3, 2):
+
+            @pl.when(in_fan(dy, i))
+            def _():
+                fan_copy(dy, i).start()
 
     def own_copy(d):
         return remote(lat_buf.at[d, j], lat_buf.at[d, j], s_own.at[d], r_own.at[d], beside)
@@ -201,16 +237,19 @@
     def q_copy(i):
         return remote(q_stage.at[(j + i) % GRP], q_buf.at[j], s_q.at[i], r_q.at[i], mate(i))
 
-    def send_far(d, carry):
-        @pl.when(g + d < groups)
-        def _():
-            far_copy(d).start()
-
-        return carry
-
     near_copy(0).start()
     own_copy(0).start()
-    lax.fori_loop(1, window + 1, send_far, 0)
+
+    @pl.when(y + 1 < SIDE)
+    def _():
+        down_copy(0).start()
+
+    fan(0)
+
+    @pl.when(corner_out)
+    def _():
+        corner_copy().start()
+
     for i in range(1, GRP):
         q_copy(i).start()
     q_buf[j] = q_stage[j]
@@ -278,14 +317,14 @@
         ws_ref[d] = jnp.sum(weighted, axis=0, keepdims=True)
 
     def spread(d):
-        @pl.when((d <= window) & (g >= d))
+        @pl.when((d <= window) & (g >= d) & (d % SIDE != 0))
         def _():
             arrived(lat_buf.at[d, j], r_far.at[d], beside)
             near_copy(d).start()
             own_copy(d).start()
 
     def hand_on(d):
-        @pl.when((d <= window) & (g >= d))
+        @pl.when((d >= 0) & (d <= window) & (g >= d))
         def _():
             arrived(lat_buf.at[d, j_near], r_near.at[d], beside)
             pass_copy(d).start()
@@ -295,6 +334,19 @@
         arrived(lat_buf.at[d, j_next], r_pass.at[d], beside)
 
     hand_on(0)
+
+    @pl.when(y >= 1)
+    def _():
+        arrived(lat_buf.at[SIDE, j], r_far.at[SIDE], beside)
+
+        @pl.when(y + 1 < SIDE)
+        def _():
+            down_copy(1).start()
+
+        near_copy(SIDE).start()
+        own_copy(SIDE).start()
+
+    fan(1)
     for i in range(1, GRP):
         arrived(q_buf.at[(j + GRP - i) % GRP], r_q.at[i], mate(i))
     blank = jnp.zeros((HALF, ROPE), BF16)
@@ -309,24 +361,32 @@
         q_lo[at + HALF : at + BLK, NOPE:] = jnp.concatenate([second, blank], axis=1)
         q_hi[at : at + HALF, NOPE:] = jnp.concatenate([blank, first], axis=1)
         q_hi[at + HALF : at + BLK, NOPE:] = jnp.concatenate([blank, second], axis=1)
-    spread(1)
     whole(0)
     scores_tile(0, True)
 
+    @pl.when(y >= 2)
+    def _():
+        arrived(lat_buf.at[2 * SIDE, j], r_far.at[2 * SIDE], beside)
+        near_copy(2 * SIDE).start()
+        own_copy(2 * SIDE).start()
+
+    fan(2)
+
     def far_scores(i, carry):
         spread(i)
-        hand_on(i - 1)
-
-        @pl.when(g >= i - 2)
-        def _():
-            whole(i - 2)
-            scores_tile(i - 2, False)
+
+        @pl.when(i > PASS_LAG)
+        def _():
+            hand_on(i - PASS_LAG)
+
+        @pl.when((i > TILE_LAG) & (g >= i - TILE_LAG))
+        def _():
+            whole(i - TILE_LAG)
+            scores_tile(i - TILE_LAG, False)
 
         return carry
 
-    spread(2)
-    hand_on(1)
-    lax.fori_loop(3, window + 3, far_scores, 0)
+    lax.fori_loop(1, window + TILE_LAG + 1, far_scores, 0)
 
     peak = jnp.max(m_ref[...], axis=0)
     factors = jnp.exp2(m_ref[...] - peak[None])
@@ -379,7 +439,15 @@
         return remote(near_send.at[d], near_recv.at[d], s_tn.at[d], r_tn.at[d], behind)
 
     def tf_copy(d):
+        return remote(far_send.at[d], far_recv.at[d], s_tf.at[d], r_tf.at[d], row_mate(4 * SIDE - d))
+
+    def tf_corner():
+        d = window
         return remote(far_send.at[d], far_recv.at[d], s_tf.at[d], r_tf.at[d], other(groups - d))
+
+    def up_copy(dy):
+        to = ((g - SIDE) * GRP + j, hz)
+        return remote(up_send.at[dy], up_recv.at[dy], s_up.at[dy], r_up.at[dy], to)
 
     def chip_sum(d):
         @pl.when((d <= window) & (g >= d))
@@ -397,7 +465,14 @@
         @pl.when((d <= window) & (g >= d))
         def _():
             far_send[d] = slot_sum(d).astype(BF16)
-            tf_copy(d).start()
+
+            @pl.when((d % SIDE != 0) & ((d < window) | (x > 0)))
+            def _():
+                tf_copy(d).start()
+
+            @pl.when((d == window) & (x == 0))
+            def _():
+                tf_corner().start()
 
     def far_grads(step, carry):
         d = window - step
@@ -408,13 +483,13 @@
             tx_copy(d).start()
             tc_copy(d).start()
 
-        chip_sum(d + 1)
-        send_terms(d + 2)
+        chip_sum(d + CHIP_LAG)
+        send_terms(d + SLOT_LAG)
         return carry
 
     lax.fori_loop(0, window + 1, far_grads, 0)
-    chip_sum(0)
-    send_terms(1)
+    for d in range(CHIP_LAG - 1, -1, -1):
+        chip_sum(d)
 
     dq_nope = (dqn[...] * SCALE).T.astype(BF16)
     dq_rope = (dqr[...] * SCALE).T.astype(BF16)
@@ -429,6 +504,43 @@
     for i in range(1, GRP):
         dq_copy(i).start()
 
+    def add(ref, sem):
+        arrived(ref, sem, beside)
+        total[...] += ref[...].astype(F32)
+
+    def row_sum(dy):
+        for i in (1, 3, 2):
+            d = SIDE * dy + (x + i) % SIDE - x
+
+            @pl.when((d >= 1) & (d <= window))
+            def _():
+                add(far_recv.at[d], r_tf.at[d])
+
+    for d in range(SLOT_LAG - 1, 3, -1):
+        send_terms(d)
+
+    @pl.when(y >= 2)
+    def _():
+        total[...] = far_send[2 * SIDE].astype(F32)
+        row_sum(2)
+        up_send[1] = total[...].astype(BF16)
+        up_copy(1).start()
+
+    for d in range(min(SLOT_LAG - 1, 3), 0, -1):
+        send_terms(d)
+
+    @pl.when(y >= 1)
+    def _():
+        total[...] = far_send[SIDE].astype(F32)
+        row_sum(1)
+
+        @pl.when(y + 1 < SIDE)
+        def _():
+            add(up_recv.at[1], r_up.at[1])
+
+        up_send[0] = total[...].astype(BF16)
+        up_copy(0).start()
+
     grad_w = dw_acc[...].T.astype(BF16)
     for i in range(groups):
         dw_send[i] = grad_w[i * w_rows : (i + 1) * w_rows]
@@ -443,16 +555,16 @@
     lax.fori_loop(1, groups, send_dw, 0)
 
     total[...] = slot_sum(0)
-
-    def take_terms(d, carry):
-        @pl.when(g + d < groups)
-        def _():
-            arrived(far_recv.at[d], r_tf.at[d], other(d))
-            total[...] += far_recv[d].astype(F32)
-
-        return carry
-
-    lax.fori_loop(1, window + 1, take_terms, 0)
+    row_sum(0)
+
+    @pl.when(corner_out)
+    def _():
+        add(far_recv.at[window], r_tf.at[window])
+
+    @pl.when(y + 1 < SIDE)
+    def _():
+        add(up_recv.at[0], r_up.at[0])
+
     for t in range(zs):
         for c in range(COLS):
             z_send[t, c * z_rows : (c + 1) * z_rows] = total[
@@ -526,10 +638,6 @@
         zf_copy(i).wait_send()
 
     def end_blocks(d, carry):
-        @pl.when((d > 0) & (g + d < groups))
-        def _():
-            far_copy(d).wait_send()
-
         @pl.when(g >= d)
         def _():
             own_copy(d).wait_send()
@@ -539,13 +647,34 @@
             tx_copy(d).wait_send()
             tn_copy(d).wait_send()
 
-        @pl.when((d > 0) & (g >= d))
+        @pl.when((d % SIDE != 0) & (g >= d))
         def _():
             tf_copy(d).wait_send()
 
         return carry
 
     lax.fori_loop(0, window + 1, end_blocks, 0)
+    for dy in range(2):
+
+        @pl.when((y + 1 < SIDE) & (y >= dy))
+        def _():
+            down_copy(dy).wait_send()
+
+        @pl.when(y > dy)
+        def _():
+            up_copy(dy).wait_send()
+
+    for dy in range(3):
+        for i in (1, 3, 2):
+
+            @pl.when(in_fan(dy, i))
+            def _():
+                fan_copy(dy, i).wait_send()
+
+    @pl.when(corner_out)
+    def _():
+        corner_copy().wait_send()
+
 
     def end_dw(i, carry):
         dw_copy(i).wait_send()
@@ -587,6 +716,8 @@
         vmem((span, PIECE, 128), BF16),
         vmem((span, PIECE, 128), BF16),
         vmem((span, PIECE, 128), BF16),
+        vmem((2, PIECE, 128), BF16),
+        vmem((2, PIECE, 128), BF16),
         vmem((PIECE, 128), F32),
         vmem((groups, w_rows, 256), BF16),
         vmem((groups, w_rows, 256), BF16),
@@ -598,7 +729,8 @@
         vmem((zs, z_piece, 128), BF16),
         vmem((zs, z_piece, 128), BF16),
     ]
-    for count in (GRP, *[span] * 8, groups, GRP, GRP, zs, zs):
+    scratch += [dma((GRP,)), dma((GRP,)), dma((2,)), dma((3, SIDE)), dma((1,)), dma((span,))]
+    for count in (*[span] * 7, 2, groups, GRP, GRP, zs, zs):
         scratch += [dma((count,)), dma((count,))]
 
     def local(query, latent, k_rope, d_out, w_kv, block_doc, block_order):

time: 107 us -> 91.6 us (0.86)
  the two profiles are of different devices: /device:TPU:16 before, /device:TPU:22 now
where the time goes in v3:
time: 91.6 us; the launch traced here: 91.4 us
  Pallas kernels  86.9 us (95%)
  local copies, waits for them, and re-layouts  3.8 us (4%)
    pallas_call x1, Pallas kernels, local(): pl.pallas_call(functools.partial(kernel, groups, zs), out_shape=(jax.Shap...  86.9 us
    unnamed x10, local copies, waits for them, and re-layouts  3.8 us

profile of v3, /device:TPU:22, one launch (start us, length us, event | category | flops | bytes accessed | tf_op | source)
XLA Modules:
  0.0 91.4 jit_solution(6049521276922793078)
XLA Ops:
  0.6 86.9 %shard_map.102 = (bf16[128,768]{1,0:T(8,128)(2,1)}, f32[128,512]{1,0:T(8,128)}, f32[64,128]{1,0:T(8,128)}, f32[8,1024]{1,0:T(8,128)}) custom-call(bf16[128,768]{1,0:T(8,128)(2,1)} %query.1, bf16[128,512]{1,0:T(8,128)(2,1)} %latent.1, bf16[64,128]{1,0:T(8,128)(2,1)} %bitcast.3, bf16[128,512]{1,0:T(8,128)(2,1)} %d_out.1, bf16[512,1024]{1,0:T(8,128)(2,1)} %w_kv.1, ...), custom_call_target="tpu_custom_call" | custom-call | tf_op jit(solution)/shard_map/pallas_call | solution.py:739
  87.5 0.0 copy-start
  87.5 1.7 %copy.15 = bf16[128,768]{1,0:T(8,128)(2,1)} copy(bf16[128,768]{1,0:T(8,128)(2,1)} %get-tuple-element.16) | data formatting | bytes 393216
  89.2 0.0 copy-done
  89.2 0.0 copy-start.2
  89.2 0.7 copy.16
  89.9 0.1 copy-done.2
  90.0 0.0 copy-start.1
  90.0 0.6 copy.17
  90.6 0.2 copy-done.1
  90.7 0.6 copy.18
Async XLA Ops:
  87.5 1.7 %copy-start = (f32[128,512]{1,0:T(8,128)S(1)}, f32[128,512]{1,0:T(8,128)}, u32[]{:S(2)}) copy-start(f32[128,512]{1,0:T(8,128)} %get-tuple-element.17) | copy-start | bytes 786436
  89.2 0.8 copy-start.2
  90.0 0.8 copy-start.1

commit v4 on v3

--- a/solution.py
+++ b/solution.py
@@ -50,6 +50,11 @@
 
 def unpack_halves(rows):
     return jnp.concatenate([rows[:, :ROPE], rows[:, ROPE:]], axis=0)
+
+
+def keep(a, b, c, d, a_out, b_out, c_out, d_out):
+    for src, dst in ((a, a_out), (b, b_out), (c, c_out), (d, d_out)):
+        dst[...] = src[...]
 
 
 def kernel(
@@ -102,6 +107,7 @@
     z_send,
     z_recv,
     z_fin,
+    s_w,
     s_q,
     r_q,
     s_down,
@@ -173,6 +179,9 @@
     def arrived(ref, sem, to):
         remote(ref, ref, sem, sem, to).wait_recv()
 
+    columns = pl.ds(pl.multiple_of(j * 256, 256), 256)
+    weights = pltpu.make_async_copy(w_kv.at[:, columns], w_head, s_w.at[0])
+    weights.start()
     barrier = pltpu.get_barrier_semaphore()
     for i in range(1, GRP):
         pl.semaphore_signal(barrier, inc=1, device_id=mate(i), device_id_type=MESH)
@@ -253,7 +262,6 @@
     for i in range(1, GRP):
         q_copy(i).start()
     q_buf[j] = q_stage[j]
-    w_head[...] = w_kv[:, pl.ds(pl.multiple_of(j * 256, 256), 256)]
 
     slot_of = lax.broadcasted_iota(jnp.int32, (1, KEYS), 1) // BLK
     in_slot = lax.broadcasted_iota(jnp.int32, (1, KEYS), 1) % BLK
@@ -362,6 +370,7 @@
         q_hi[at : at + HALF, NOPE:] = jnp.concatenate([blank, first], axis=1)
         q_hi[at + HALF : at + BLK, NOPE:] = jnp.concatenate([blank, second], axis=1)
     whole(0)
+    weights.wait()
     scores_tile(0, True)
 
     @pl.when(y >= 2)
@@ -729,14 +738,15 @@
         vmem((zs, z_piece, 128), BF16),
         vmem((zs, z_piece, 128), BF16),
     ]
-    scratch += [dma((GRP,)), dma((GRP,)), dma((2,)), dma((3, SIDE)), dma((1,)), dma((span,))]
+    scratch += [dma((1,)), dma((GRP,)), dma((GRP,)), dma((2,)), dma((3, SIDE)), dma((1,)), dma((span,))]
     for count in (*[span] * 7, 2, groups, GRP, GRP, zs, zs):
         scratch += [dma((count,)), dma((count,))]
 
     def local(query, latent, k_rope, d_out, w_kv, block_doc, block_order):
         whole = pl.BlockSpec(memory_space=pltpu.VMEM)
         scalars = pl.BlockSpec(memory_space=pltpu.SMEM)
-        d_query, d_latent, d_rope, d_w_kv = pl.pallas_call(
+        anywhere = pl.BlockSpec(memory_space=pl.ANY)
+        results = pl.pallas_call(
             functools.partial(kernel, groups, zs),
             out_shape=(
                 jax.ShapeDtypeStruct(query.shape, BF16),
@@ -744,13 +754,19 @@
                 jax.ShapeDtypeStruct((ROPE, BLK), F32),
                 jax.ShapeDtypeStruct((w_rows // GRP, GRP * 256), F32),
             ),
-            in_specs=[whole] * 5 + [scalars] * 2,
+            in_specs=[whole] * 4 + [anywhere] + [scalars] * 2,
             out_specs=(whole,) * 4,
             scratch_shapes=scratch,
             compiler_params=pltpu.CompilerParams(
                 collective_id=0, has_side_effects=True, vmem_limit_bytes=56 * 1024 * 1024
             ),
         )(query, latent, k_rope.T, d_out, w_kv, block_doc, block_order)
+        d_query, d_latent, d_rope, d_w_kv = pl.pallas_call(
+            keep,
+            out_shape=tuple(jax.ShapeDtypeStruct(r.shape, r.dtype) for r in results),
+            in_specs=[whole] * 4,
+            out_specs=(whole,) * 4,
+        )(*results)
         return d_query, d_latent, d_rope.T, d_w_kv
 
     return jax.shard_map(

time: 91.6 us -> 89.1 us (0.973)
  local copies, waits for them, and re-layouts: 3.8 us -> 0 us
  Pallas kernels: 86.9 us -> 88.3 us
    unnamed x10 -> x0, local copies, waits for them, and re-layouts: 3.8 us -> none
    pallas_call x0 -> x1, Pallas kernels: none -> 1.81 us  [local(): pl.pallas_call(keep, out_shape=tuple((jax.ShapeDtypeStruct(r.shape, r.dty...]
where the time goes in v4:
time: 89.1 us; the launch traced here: 89 us
  Pallas kernels  88.3 us (99%)
    pallas_call x1, Pallas kernels, local(): pl.pallas_call(functools.partial(kernel, groups, zs), out_shape=(jax.Shap...  86.5 us
    pallas_call x1, Pallas kernels, local(): pl.pallas_call(keep, out_shape=tuple((jax.ShapeDtypeStruct(r.shape, r.dty...  1.81 us

profile of v4, /device:TPU:22, one launch (start us, length us, event | category | flops | bytes accessed | tf_op | source)
XLA Modules:
  0.0 89.0 jit_solution(13012419782667276198)
XLA Ops:
  0.6 86.5 %shard_map.102 = (bf16[128,768]{1,0:T(8,128)(2,1)}, f32[128,512]{1,0:T(8,128)}, f32[64,128]{1,0:T(8,128)}, f32[8,1024]{1,0:T(8,128)}) custom-call(bf16[128,768]{1,0:T(8,128)(2,1)} %query.1, bf16[128,512]{1,0:T(8,128)(2,1)} %latent.1, bf16[64,128]{1,0:T(8,128)(2,1)} %bitcast.2, bf16[128,512]{1,0:T(8,128)(2,1)} %d_out.1, bf16[512,1024]{1,0:T(8,128)(2,1)} %w_kv.1, ...), custom_call_target="tpu_custom_call" | custom-call | tf_op jit(solution)/shard_map/pallas_call | solution.py:749
  87.2 1.8 %shard_map.103 = (bf16[128,768]{1,0:T(8,128)(2,1)}, f32[128,512]{1,0:T(8,128)}, f32[64,128]{1,0:T(8,128)}, f32[8,1024]{1,0:T(8,128)}) custom-call(bf16[128,768]{1,0:T(8,128)(2,1)} %get-tuple-element.12.a, f32[128,512]{1,0:T(8,128)} %get-tuple-element.13.b, f32[64,128]{1,0:T(8,128)} %get-tuple-element.14.c, f32[8,1024]{1,0:T(8,128)} %get-tuple-element.15.d), custom_call_target="tpu_custom_call" | custom-call | tf_op jit(solution)/shard_map/pallas_call | solution.py:764

commit v5 on v4

--- a/solution.py
+++ b/solution.py
@@ -22,7 +22,7 @@
 COLS = LAT // BLK
 PIECE = LAT + HALF
 PASS_LAG, TILE_LAG = 3, 5
-CHIP_LAG, SLOT_LAG = 1, 4
+CHIP_LAG, SLOT_LAG = 2, 5
 MOST = 36
 SCALE = HEAD**-0.5
 LOG2E = math.log2(math.e)

time: 89.1 us -> 88.6 us (level)
  no operation moved by 1% of the time
where the time goes in v5:
time: 88.6 us; the launch traced here: 88.2 us
  Pallas kernels  87.6 us (99%)
    pallas_call x1, Pallas kernels, local(): pl.pallas_call(functools.partial(kernel, groups, zs), out_shape=(jax.Shap...  85.8 us
    pallas_call x1, Pallas kernels, local(): pl.pallas_call(keep, out_shape=tuple((jax.ShapeDtypeStruct(r.shape, r.dty...  1.81 us

profile of v5, /device:TPU:22, one launch (start us, length us, event | category | flops | bytes accessed | tf_op | source)
XLA Modules:
  0.0 88.2 jit_solution(14353123763999302605)
XLA Ops:
  0.6 85.8 %shard_map.102 = (bf16[128,768]{1,0:T(8,128)(2,1)}, f32[128,512]{1,0:T(8,128)}, f32[64,128]{1,0:T(8,128)}, f32[8,1024]{1,0:T(8,128)}) custom-call(bf16[128,768]{1,0:T(8,128)(2,1)} %query.1, bf16[128,512]{1,0:T(8,128)(2,1)} %latent.1, bf16[64,128]{1,0:T(8,128)(2,1)} %bitcast.2, bf16[128,512]{1,0:T(8,128)(2,1)} %d_out.1, bf16[512,1024]{1,0:T(8,128)(2,1)} %w_kv.1, ...), custom_call_target="tpu_custom_call" | custom-call | tf_op jit(solution)/shard_map/pallas_call | solution.py:749
  86.4 1.8 %shard_map.103 = (bf16[128,768]{1,0:T(8,128)(2,1)}, f32[128,512]{1,0:T(8,128)}, f32[64,128]{1,0:T(8,128)}, f32[8,1024]{1,0:T(8,128)}) custom-call(bf16[128,768]{1,0:T(8,128)(2,1)} %get-tuple-element.12.a, f32[128,512]{1,0:T(8,128)} %get-tuple-element.13.b, f32[64,128]{1,0:T(8,128)} %get-tuple-element.14.c, f32[8,1024]{1,0:T(8,128)} %get-tuple-element.15.d), custom_call_target="tpu_custom_call" | custom-call | tf_op jit(solution)/shard_map/pallas_call | solution.py:764

commit v6 on v5

--- a/solution.py
+++ b/solution.py
@@ -588,6 +588,49 @@
         z_copy(i).start()
 
     for i in range(1, GRP):
+        q_copy(i).wait_send()
+        dq_copy(i).wait_send()
+
+    def end_blocks(d, carry):
+        @pl.when(g >= d)
+        def _():
+            own_copy(d).wait_send()
+            near_copy(d).wait_send()
+            pass_copy(d).wait_send()
+            tc_copy(d).wait_send()
+            tx_copy(d).wait_send()
+            tn_copy(d).wait_send()
+
+        @pl.when((d % SIDE != 0) & (g >= d))
+        def _():
+            tf_copy(d).wait_send()
+
+        return carry
+
+    lax.fori_loop(0, window + 1, end_blocks, 0)
+    for dy in range(2):
+
+        @pl.when((y + 1 < SIDE) & (y >= dy))
+        def _():
+            down_copy(dy).wait_send()
+
+        @pl.when(y > dy)
+        def _():
+            up_copy(dy).wait_send()
+
+    for dy in range(3):
+        for i in (1, 3, 2):
+
+            @pl.when(in_fan(dy, i))
+            def _():
+                fan_copy(dy, i).wait_send()
+
+    @pl.when(corner_out)
+    def _():
+        corner_copy().wait_send()
+
+
+    for i in range(1, GRP):
         arrived(dq_recv.at[(j + GRP - i) % GRP], r_dq.at[i], mate(i))
     columns = []
     for h in range(GRP):
@@ -639,51 +682,10 @@
     dw_out[...] = jnp.concatenate([dw_fin[h] for h in range(GRP)], axis=1)
 
     for i in range(1, GRP):
-        q_copy(i).wait_send()
-        dq_copy(i).wait_send()
         dwf_copy(i).wait_send()
     for i in range(1, zs):
         z_copy(i).wait_send()
         zf_copy(i).wait_send()
-
-    def end_blocks(d, carry):
-        @pl.when(g >= d)
-        def _():
-            own_copy(d).wait_send()
-            near_copy(d).wait_send()
-            pass_copy(d).wait_send()
-            tc_copy(d).wait_send()
-            tx_copy(d).wait_send()
-            tn_copy(d).wait_send()
-
-        @pl.when((d % SIDE != 0) & (g >= d))
-        def _():
-            tf_copy(d).wait_send()
-
-        return carry
-
-    lax.fori_loop(0, window + 1, end_blocks, 0)
-    for dy in range(2):
-
-        @pl.when((y + 1 < SIDE) & (y >= dy))
-        def _():
-            down_copy(dy).wait_send()
-
-        @pl.when(y > dy)
-        def _():
-            up_copy(dy).wait_send()
-
-    for dy in range(3):
-        for i in (1, 3, 2):
-
-            @pl.when(in_fan(dy, i))
-            def _():
-                fan_copy(dy, i).wait_send()
-
-    @pl.when(corner_out)
-    def _():
-        corner_copy().wait_send()
-
 
     def end_dw(i, carry):
         dw_copy(i).wait_send()

time: 88.6 us -> 88.4 us (level)
  no operation moved by 1% of the time
where the time goes in v6:
time: 88.4 us; the launch traced here: 88 us
  Pallas kernels  87.3 us (99%)
    pallas_call x1, Pallas kernels, local(): pl.pallas_call(functools.partial(kernel, groups, zs), out_shape=(jax.Shap...  85.5 us
    pallas_call x1, Pallas kernels, local(): pl.pallas_call(keep, out_shape=tuple((jax.ShapeDtypeStruct(r.shape, r.dty...  1.81 us

profile of v6, /device:TPU:22, one launch (start us, length us, event | category | flops | bytes accessed | tf_op | source)
XLA Modules:
  0.0 88.0 jit_solution(11597912158264736166)
XLA Ops:
  0.6 85.5 %shard_map.102 = (bf16[128,768]{1,0:T(8,128)(2,1)}, f32[128,512]{1,0:T(8,128)}, f32[64,128]{1,0:T(8,128)}, f32[8,1024]{1,0:T(8,128)}) custom-call(bf16[128,768]{1,0:T(8,128)(2,1)} %query.1, bf16[128,512]{1,0:T(8,128)(2,1)} %latent.1, bf16[64,128]{1,0:T(8,128)(2,1)} %bitcast.2, bf16[128,512]{1,0:T(8,128)(2,1)} %d_out.1, bf16[512,1024]{1,0:T(8,128)(2,1)} %w_kv.1, ...), custom_call_target="tpu_custom_call" | custom-call | tf_op jit(solution)/shard_map/pallas_call | solution.py:751
  86.1 1.8 %shard_map.103 = (bf16[128,768]{1,0:T(8,128)(2,1)}, f32[128,512]{1,0:T(8,128)}, f32[64,128]{1,0:T(8,128)}, f32[8,1024]{1,0:T(8,128)}) custom-call(bf16[128,768]{1,0:T(8,128)(2,1)} %get-tuple-element.12.a, f32[128,512]{1,0:T(8,128)} %get-tuple-element.13.b, f32[64,128]{1,0:T(8,128)} %get-tuple-element.14.c, f32[8,1024]{1,0:T(8,128)} %get-tuple-element.15.d), custom_call_target="tpu_custom_call" | custom-call | tf_op jit(solution)/shard_map/pallas_call | solution.py:766
